TPU v7x, 32 devices: a whole 2x2x4 slice. The times are simulated.
32 devices in a mesh: grp: 2 (over y), blk: 4 (over z), col: 2 (over x), rep: 2 (over core).
Axes of the slice: x: 2, y: 2, z: 4, core: 2. Of those that a mesh axis runs over, the one named last changes fastest.
Arguments:
- coords: float32 [3, 131072], P(None, ('grp', 'blk')), parts along dimension 1, may hold values from 0 to 1
- observations: float32 [131072], P(('grp', 'blk')), parts along dimension 0, may hold values from -6 to 6
- nugget: float32 [131072], P(('grp', 'blk')), parts along dimension 0, may hold values from 0.1 to 1
- tile_pairs: int32 [2, 8192], P(None, ('grp', 'blk', 'col', 'rep')), parts along dimension 1, may hold values from 0 to 511, as said below
- tile_live: int32 [32], P(('grp', 'blk', 'col', 'rep')), parts along dimension 0, may hold values from 64 to 256, as said below
Outputs:
- solution_field: float32 [131072], P(('grp', 'blk')), parts along dimension 0
- residual: float32 [131072], P(('grp', 'blk')), parts along dimension 0
There are 2 independent parts, one for each index of `grp`. A program takes and returns all parts, laid end to end along the dimension named above; each array names one. Nothing has to cross between parts.
Inputs may be any that keep to these rules, and one draw needn't show every extreme that they name: `tile_pairs`: entries name point blocks. Every slot has its row block, or else its column block, among the 128 blocks of its own device's index of blk; most slots have the row block there. Call the slot's other block its column block when the row block is the device's own, else its row block. Of one device's slots, at most (259) // 4 have their other block among the blocks of any one index of blk, and on every device some index gets exactly that many. Slots at or beyond a device's live count are ignored. `tile_live`: some device has all 256 slots live.
All inputs are finite; a program needn't handle non-finite values.
Results may differ from a plain program's by a relative error of at most 0.0003.
Values sent between devices are 32-bit elements; how exact they have to be, the bound alone decides.
No kernel may reach another device: no remote copies, remote signals or barrier semaphores. Data moves between devices by JAX's collectives and lax.ppermute only.
A program may use at most 128 MiB of HBM per device.

v0:
```python
import functools

import jax
import jax.numpy as jnp
from jax import lax
from jax.experimental import pallas as pl
from jax.experimental.pallas import tpu as pltpu
from jax.sharding import PartitionSpec as P

BS = 128
ITERS = 3
SUPPORT = 0.3
DEPTH = 48
UNROLL = 4
ARRAYS = 4
MIB = 1024 * 1024
EVERY = ("blk", "col", "rep")
PLANE = ("col", "rep")
VMEM = pl.BlockSpec(memory_space=pltpu.VMEM)
SMEM = pl.BlockSpec(memory_space=pltpu.SMEM)
ANY = pl.BlockSpec(memory_space=pl.ANY)
BF16 = jnp.bfloat16
F32 = jnp.float32


class Sizes:
    def __init__(self, points, slots):
        self.blks = lax.axis_size("blk")
        self.reps = lax.axis_size("rep")
        self.plane = lax.axis_size("col") * self.reps
        self.devs = self.blks * self.plane
        self.points = points
        self.slots = slots
        self.local_blocks = points // BS
        self.blocks = self.local_blocks * self.blks
        self.own = self.local_blocks // self.plane
        self.capacity = 2 * self.plane * slots
        per_row = slots * self.devs // self.blocks
        self.first_mib = 6 + self.blocks * DEPTH * BS * 2 // MIB
        self.kept = min(448, (48 - self.first_mib) * 16) // ARRAYS
        self.scale = 16.0 / (BS * per_row) / 256.0

    def me(self):
        return (lax.axis_index("blk") * lax.axis_size("col") + lax.axis_index("col")) * self.reps + lax.axis_index(
            "rep"
        )


def exchange(x, axes):
    return lax.all_to_all(x, axes, split_axis=0, concat_axis=0, tiled=True)


def copies(x, count):
    return jnp.broadcast_to(x[None], (count,) + x.shape).reshape((count * x.shape[0],) + x.shape[1:])


def split3(x):
    high = x.astype(BF16).astype(F32)
    rest = x - high
    middle = rest.astype(BF16).astype(F32)
    return high, middle, rest - middle


def lhs_kernel(sz, coords_ref, out_ref):
    quarter = lax.axis_index("col") * sz.reps + lax.axis_index("rep")
    unit = jnp.ones((1, BS), F32)
    for i in range(sz.own):
        start = pl.multiple_of((quarter * sz.own + i) * BS, BS)
        x = (coords_ref[:, pl.ds(start, BS)] - 0.5) * (4.0 / SUPPORT)
        norm = jnp.sum(x * x, axis=0, keepdims=True)
        h, m, l = split3(jnp.concatenate([x, unit, norm, jnp.zeros((3, BS), F32)], axis=0))
        feats = jnp.concatenate([h, h, m, m, h, l, jnp.zeros((BS - DEPTH, BS), F32)], axis=0)
        out_ref[i * BS : (i + 1) * BS, :] = feats.T.astype(BF16)
    out_ref[sz.own * BS :, :] = jnp.zeros((BS, BS), BF16)


def list_kernel(sz, pairs_ref, out_ref, count_ref, target, other, place, value, key_column, key_row, entry_row):
    me = sz.me()
    lines = sz.slots // BS
    at = 2 * lines * sz.devs
    for base in range(0, at, 2 * lines):
        rows = pairs_ref[base : base + lines, :]
        cols = pairs_ref[base + lines : base + 2 * lines, :]
        target[base : base + lines, :] = rows
        other[base : base + lines, :] = cols
        target[base + lines : base + 2 * lines, :] = cols
        other[base + lines : base + 2 * lines, :] = rows
    local = target[...] - me * sz.own
    mine = jnp.logical_and(local >= 0, local < sz.own)
    flags = jnp.where(mine, 1.0, 0.0)
    a = lax.broadcasted_iota(jnp.int32, (BS, BS), 0)
    b = lax.broadcasted_iota(jnp.int32, (BS, BS), 1)
    before = jnp.dot(flags.astype(BF16), jnp.where(a < b, 1.0, 0.0).astype(BF16), preferred_element_type=F32)
    totals = jnp.broadcast_to(jnp.sum(flags, axis=1, keepdims=True), (at, BS))
    a = lax.broadcasted_iota(jnp.int32, (at, at), 0)
    b = lax.broadcasted_iota(jnp.int32, (at, at), 1)
    above = jnp.dot(jnp.where(b < a, 1.0, 0.0).astype(BF16), totals.astype(BF16), preferred_element_type=F32)
    place[...] = jnp.where(mine, above + before, -1.0)
    value[...] = (local + 256 * other[...]).astype(F32)
    count = jnp.sum(flags).astype(jnp.int32)
    count_ref[0] = count
    sub = lax.broadcasted_iota(jnp.int32, (BS, BS), 0)
    lane = lax.broadcasted_iota(jnp.int32, (1, BS), 1)

    chunks = lax.shift_right_logical(count + BS - 1, 7)

    def key_of(found, slot):
        entry = jnp.where(slot < count, found.astype(jnp.int32), sz.own)
        return entry.astype(F32), (jnp.bitwise_and(entry, 255) * 65536 + slot).astype(F32)

    def compact(c, unused):
        slot = (sub + c * BS).astype(F32)

        def line(r, total):
            hit = place[pl.ds(r, 1), :] == slot
            return total + jnp.where(hit, value[pl.ds(r, 1), :], 0.0)

        total = lax.fori_loop(0, at, line, jnp.zeros((BS, BS), F32), unroll=4)
        entry, key = key_of(jnp.sum(total.T, axis=0, keepdims=True), lane + c * BS)
        entry_row[pl.ds(c, 1), :] = entry
        key_row[pl.ds(c, 1), :] = key
        unused_entry, key = key_of(jnp.sum(total, axis=1, keepdims=True), sub[:, 0:1] + c * BS)
        key_column[pl.ds(pl.multiple_of(c * BS, BS), BS), :] = jnp.broadcast_to(key, (BS, BS))
        return unused

    lax.fori_loop(0, chunks, compact, 0)

    def rank(c, unused):
        def below(k, total):
            lower = key_column[pl.ds(pl.multiple_of(k * BS, BS), BS), :] < key_row[pl.ds(c, 1), :]
            return total + jnp.where(lower, 1.0, 0.0)

        total = lax.fori_loop(0, chunks, below, jnp.zeros((BS, BS), F32))
        place[pl.ds(c, 1), :] = jnp.sum(total, axis=0, keepdims=True)
        return unused

    lax.fori_loop(0, chunks, rank, 0)

    def arrange(c, unused):
        slot = (sub + c * BS).astype(F32)

        def line(r, total):
            hit = place[pl.ds(r, 1), :] == slot
            return total + jnp.where(hit, entry_row[pl.ds(r, 1), :], 0.0)

        total = lax.fori_loop(0, chunks, line, jnp.zeros((BS, BS), F32))
        out_ref[pl.ds(c, 1), :] = jnp.sum(total.T, axis=0, keepdims=True).astype(jnp.int32)
        return unused

    lax.fori_loop(0, chunks, arrange, 0)


def entry_of(list_ref, k):
    entry = list_ref[k]
    return jnp.bitwise_and(entry, 255), lax.shift_right_logical(entry, 8)


def tile_of(features, other_features):
    squared = jnp.maximum(jnp.dot(features, other_features, preferred_element_type=F32), 1e-20)
    remain = jnp.maximum(4.0 - squared * lax.rsqrt(squared), 0.0)
    twice = remain * remain
    return twice * twice * (5.0 - remain)


def kept_groups(sz, count, at):
    first = at * (sz.kept // UNROLL)
    last = jnp.minimum(lax.div(count + (UNROLL - 1), UNROLL), first + sz.kept // UNROLL)
    return first, jnp.maximum(first, last)


def generate(sz, list_ref, count, lhs_ref, rhs_ref, tile_refs):
    for at, tile_ref in enumerate(tile_refs):

        def group(g, unused, at=at, tile_ref=tile_ref):
            for u in range(UNROLL):
                i, j = entry_of(list_ref, g * UNROLL + u)
                start = pl.multiple_of((g * UNROLL + u - at * sz.kept) * BS, BS)
                tile_ref[pl.ds(start, BS), :] = tile_of(
                    lhs_ref[pl.ds(pl.multiple_of(i * BS, BS), BS), :DEPTH],
                    rhs_ref[pl.ds(pl.multiple_of(j * DEPTH, DEPTH), DEPTH), :],
                )
            return unused

        lax.fori_loop(*kept_groups(sz, count, at), group, 0)


def sweep(sz, list_ref, count, tile_refs, vec_ref, acc, acc_ones, remake):
    accs = [acc] if acc_ones is None else [acc, acc_ones]
    for ref in accs:
        ref[...] = jnp.zeros_like(ref)
    carry = (jnp.int32(-1),) + tuple(jnp.zeros((BS, BS), F32) for unused in accs)
    for at, tile_ref in enumerate(tile_refs):

        def group(g, carry, at=at, tile_ref=tile_ref):
            before, *sums = carry
            for u in range(UNROLL):
                i, j = entry_of(list_ref, g * UNROLL + u)
                keep = jnp.where(i == before, 1.0, 0.0)
                start = pl.multiple_of((g * UNROLL + u - at * sz.kept) * BS, BS)
                tile = tile_ref[pl.ds(start, BS), :]
                terms = [tile * vec_ref[pl.ds(j, 1), :], tile]
                sums = [total * keep + term for total, term in zip(sums, terms)]
                for ref, total in zip(accs, sums):
                    ref[pl.ds(pl.multiple_of(i * BS, BS), BS), :] = total
                before = i
            return (before, *sums)

        carry = lax.fori_loop(*kept_groups(sz, count, at), group, carry)

    def extra(k, unused):
        i, j = entry_of(list_ref, k)
        tile = tile_of(*remake(i, j))
        rows = pl.ds(pl.multiple_of(i * BS, BS), BS)
        acc[rows, :] += tile * vec_ref[pl.ds(j, 1), :]
        if acc_ones is not None:
            acc_ones[rows, :] += tile
        return unused

    kept = sz.kept * len(tile_refs)
    lax.fori_loop(kept, jnp.maximum(count, kept), extra, 0)


def finish(sz, acc, out_ref):
    unit = jnp.ones((8, BS), BF16)
    across = (((1,), (1,)), ((), ()))
    for i in range(sz.own):
        whole = acc[i * BS : (i + 1) * BS, :]
        high = whole.astype(BF16)
        low = (whole - high.astype(F32)).astype(BF16)
        y = lax.dot_general(unit, high, across, preferred_element_type=F32)
        y = y + lax.dot_general(unit, low, across, preferred_element_type=F32)
        out_ref[i : i + 1, :] = y[0:1, :] * sz.scale


def fan_out(ref, rows, value):
    for k in range(ref.shape[0] // rows):
        ref[k * rows : (k + 1) * rows, :] = value


def total_of(x):
    return jnp.sum(jnp.sum(x, axis=0, keepdims=True), axis=1, keepdims=True)


def first_kernel(sz, *refs):
    list_ref, count_ref, lhs_ref, nugget_ref, obs_home_ref, near_ref, far_ref = refs[:7]
    tile_refs = refs[7 : 7 + ARRAYS]
    spare_ref, obs_ref, diag_ref, mapped_ref, norm_ref, rhs_ref, acc, acc_ones, total_row, done = refs[7 + ARRAYS :]
    rep = lax.axis_index("rep")
    part = sz.local_blocks // sz.reps
    feature = lax.broadcasted_iota(jnp.int32, (8, BS), 0)
    for piece_ref, turn in ((near_ref, 0), (far_ref, 1)):
        for z in range(sz.blks):
            base = z * 4 * part
            first = pl.multiple_of(z * sz.local_blocks + jnp.bitwise_xor(rep, turn) * part, 8)
            obs_ref[pl.ds(first, part), :] = piece_ref[base + 3 * part : base + 4 * part, :]

            def one(k, unused, base=base, first=first, piece_ref=piece_ref):
                x, y, z = ((piece_ref[pl.ds(base + c * part + k, 1), :] - 0.5) * (4.0 / SUPPORT) for c in range(3))
                feats = jnp.where(feature == 4, 1.0, 0.0)
                for place, row in enumerate((-2.0 * x, -2.0 * y, -2.0 * z, x * x + y * y + z * z)):
                    feats = jnp.where(feature == place, row, feats)
                h, m, l = split3(feats)
                feats = jnp.concatenate([h, m, h, m, l, h], axis=0).astype(BF16)
                rhs_ref[pl.ds(pl.multiple_of((first + k) * DEPTH, DEPTH), DEPTH), :] = feats
                return unused

            lax.fori_loop(0, part, one, 0, unroll=4)
    count = count_ref[0]
    generate(sz, list_ref, count, lhs_ref, rhs_ref, tile_refs)

    def remake(i, j):
        features = lhs_ref[pl.ds(pl.multiple_of(i * BS, BS), BS), :DEPTH]
        return features, rhs_ref[pl.ds(pl.multiple_of(j * DEPTH, DEPTH), DEPTH), :]

    sweep(sz, list_ref, count, tile_refs, obs_ref, acc, acc_ones, remake)

    @pl.when(count > sz.kept * ARRAYS)
    def save():
        copy = pltpu.make_async_copy(rhs_ref, spare_ref, done)
        copy.start()
        copy.wait()

    finish(sz, acc_ones, total_row)
    finish(sz, acc, mapped_ref)
    quarter = lax.axis_index("col") * sz.reps + rep
    own = pl.ds(pl.multiple_of(sz.me() * sz.own, 8), sz.own)
    diag = nugget_ref[pl.ds(pl.multiple_of(quarter * sz.own, 8), sz.own), :] + total_row[...]
    diag_ref[...] = diag
    fan_out(mapped_ref, sz.own, mapped_ref[: sz.own, :] + diag * obs_ref[own, :])
    norm_ref[...] = jnp.broadcast_to(total_of(obs_ref[...] * obs_ref[...]), (8, BS))


def step_kernel(sz, last, *refs):
    list_ref, count_ref, lhs_ref, spare_ref, diag_ref, norm_ref, field_ref, resid_ref, dirn_ref, mapped = refs[:10]
    tile_refs = refs[10 : 10 + ARRAYS]
    rest = refs[10 + ARRAYS :]
    mapped_ref, next_norm_ref, next_field_ref, next_resid_ref, next_dirn_ref = rest[:5]
    if last:
        dot_ref, dirn = rest[5:7]
    else:
        dirn = next_dirn_ref
    acc, features, others, done = rest[-4:]
    me = sz.me()
    norm = norm_ref[0:1, 0:1]
    step = norm / total_of(dirn_ref[...] * mapped[...])
    resid = resid_ref[...] - step * mapped[...]
    next_norm = total_of(resid * resid)
    dirn[...] = resid + (next_norm / norm) * dirn_ref[...]
    next_norm_ref[...] = jnp.broadcast_to(next_norm, (8, BS))
    home = pl.ds(pl.multiple_of(lax.axis_index("blk") * sz.local_blocks, 8), sz.local_blocks)
    own = pl.ds(pl.multiple_of(me * sz.own, 8), sz.own)
    field = step * dirn_ref[home, :]
    if last:
        next_field_ref[...] = field_ref[...] + field
        next_resid_ref[...] = resid_ref[home, :] - step * mapped[home, :]
        next_dirn_ref[...] = dirn[home, :]
    else:
        next_field_ref[...] = field
        next_resid_ref[...] = resid

    def remake(i, j):
        for source, start, size, target in ((lhs_ref, i, BS, features), (spare_ref, j, DEPTH, others)):
            copy = pltpu.make_async_copy(source.at[pl.ds(pl.multiple_of(start * size, size), size), :], target, done)
            copy.start()
            copy.wait()
        return features[:, :DEPTH], others[...]

    sweep(sz, list_ref, count_ref[0], tile_refs, dirn, acc, None, remake)
    finish(sz, acc, mapped_ref)
    ours = mapped_ref[: sz.own, :] + diag_ref[...] * dirn[own, :]
    fan_out(mapped_ref, sz.own, ours)
    if last:
        dot_ref[...] = jnp.broadcast_to(total_of(ours * dirn[own, :]), dot_ref.shape)


def last_kernel(sz, norm_ref, field_ref, resid_ref, dirn_ref, mapped_ref, dot_ref, out_field_ref, out_resid_ref):
    product = jnp.sum(dot_ref[...], axis=0, keepdims=True) * 0.125
    step = norm_ref[0:1, :] / product
    out_field_ref[...] = field_ref[...] + step * dirn_ref[...]
    out_resid_ref[...] = resid_ref[...] - step * mapped_ref[...]


def call(kernel, mib, in_specs, shapes, out_specs, scratch, flops, *args):
    return pl.pallas_call(
        kernel,
        in_specs=in_specs,
        out_shape=shapes,
        out_specs=out_specs,
        scratch_shapes=scratch,
        compiler_params=pltpu.CompilerParams(vmem_limit_bytes=mib * MIB),
        cost_estimate=pl.CostEstimate(flops=flops, bytes_accessed=1 << 20, transcendentals=0),
    )(*args)


def array(*shape, dtype=F32):
    return jax.ShapeDtypeStruct(shape, dtype)


def local(coords, observations, nugget, tile_pairs, tile_live):
    sz = Sizes(observations.shape[0], tile_pairs.shape[1])
    own, blocks, home = sz.own, sz.blocks, sz.local_blocks
    alive = jnp.arange(sz.slots, dtype=jnp.int32) < tile_live[0]
    pairs = jnp.where(alive, tile_pairs, -1).reshape(2 * sz.slots // BS, BS)
    pairs = exchange(copies(pairs, sz.devs), EVERY)

    rep = lax.axis_index("rep")
    obs_rows = observations.reshape(home, BS)
    half = sz.points // sz.reps
    payload = jnp.concatenate([coords, observations[None]], axis=0)
    payload = lax.dynamic_slice_in_dim(payload, rep * half, half, axis=1)
    near = exchange(copies(payload.reshape(4 * home // sz.reps, BS), sz.blks), "blk")
    far = lax.ppermute(near, "rep", [(i, i ^ 1) for i in range(sz.reps)])

    lhs = call(
        functools.partial(lhs_kernel, sz),
        12,
        [VMEM],
        array((own + 1) * BS, BS, dtype=BF16),
        VMEM,
        [],
        10_000_000,
        coords,
    )
    lines = 2 * sz.slots // BS * sz.devs
    table, count = call(
        functools.partial(list_kernel, sz),
        12,
        [VMEM],
        (array(sz.capacity // BS, BS, dtype=jnp.int32), array(1, dtype=jnp.int32)),
        (VMEM, SMEM),
        [pltpu.VMEM((lines, BS), jnp.int32)] * 2
        + [pltpu.VMEM((lines, BS), F32)] * 2
        + [pltpu.VMEM((sz.capacity, BS), F32)]
        + [pltpu.VMEM((sz.capacity // BS, BS), F32)] * 2,
        10_000_000,
        pairs,
    )
    table = table.reshape(sz.capacity)
    tall = pltpu.VMEM(((own + 1) * BS, BS), F32)
    kept = [pltpu.VMEM((sz.kept * BS, BS), F32)] * ARRAYS
    *tiles, spare, obs, diag, mapped, norm = call(
        functools.partial(first_kernel, sz),
        sz.first_mib,
        [SMEM, SMEM] + [VMEM] * 5,
        kept
        + [
            pltpu.HBM((blocks * DEPTH, BS), BF16),
            array(blocks, BS),
            array(own, BS),
            array(sz.devs * own, BS),
            array(8, BS),
        ],
        [VMEM] * ARRAYS + [ANY] + [VMEM] * 4,
        [
            pltpu.VMEM((blocks * DEPTH, BS), BF16),
            tall,
            tall,
            pltpu.VMEM((own, BS), F32),
            pltpu.SemaphoreType.DMA,
        ],
        100_000_000,
        table,
        count,
        lhs,
        nugget.reshape(home, BS),
        obs_rows,
        near,
        far,
    )
    tiles = [pltpu.with_memory_space_constraint(tile, pltpu.VMEM) for tile in tiles]
    spare = pltpu.with_memory_space_constraint(spare, pltpu.HBM)
    field, resid, dirn = norm, obs, obs
    for sweep_index in range(1, ITERS):
        last = sweep_index + 1 == ITERS
        span = home if last else blocks
        peers = sz.plane if last else sz.devs
        outs = [array(peers * own, BS), array(8, BS), array(home, BS), array(span, BS), array(span, BS)]
        mapped, norm, field, resid, dirn, *dot = call(
            functools.partial(step_kernel, sz, last),
            5,
            [SMEM, SMEM, ANY, ANY] + [VMEM] * (6 + ARRAYS),
            outs + [array(8 * sz.devs, BS)] * last,
            [VMEM] * (len(outs) + last),
            [pltpu.VMEM((blocks, BS), F32)] * last
            + [tall, pltpu.VMEM((BS, BS), BF16), pltpu.VMEM((DEPTH, BS), BF16), pltpu.SemaphoreType.DMA],
            100_000_000,
            table,
            count,
            lhs,
            spare,
            diag,
            norm,
            field,
            resid,
            dirn,
            exchange(mapped, EVERY),
            *tiles,
        )
    field, resid = call(
        functools.partial(last_kernel, sz),
        4,
        [VMEM] * 6,
        (array(home, BS), array(home, BS)),
        (VMEM, VMEM),
        [],
        100_000,
        norm,
        field,
        resid,
        dirn,
        exchange(mapped, PLANE),
        exchange(dot[0], EVERY),
    )
    return field.reshape(sz.points), resid.reshape(sz.points)


def solution(mesh):
    in_specs = (
        P(None, ("grp", "blk")),
        P(("grp", "blk")),
        P(("grp", "blk")),
        P(None, ("grp", "blk", "col", "rep")),
        P(("grp", "blk", "col", "rep")),
    )
    out_specs = (P(("grp", "blk")), P(("grp", "blk")))
    return jax.shard_map(local, mesh=mesh, in_specs=in_specs, out_specs=out_specs, check_vma=False)
```

profile of v0, /device:TPU:0, one launch (start us, length us, event | category | flops | bytes accessed | tf_op | source)
XLA Modules:
  0.0 135.3 jit_solution(107026609430807867)
XLA Ops:
  0.6 1.0 fusion
  1.7 0.1 broadcast_in_dim.30
  1.8 20.6 %all_to_all.60 = f32[4,256,128]{2,1,0:T(8,128)S(1)} all-to-all(f32[4,256,128]{2,1,0:T(8,128)S(1)} %broadcast_in_dim.31), channel_id=1, replica_groups=mesh['grp'=2,'blk'=4,'col'=2,'rep'=2] {'blk'}, dimensions={0} | all-to-all | bytes 1048576 | tf_op jit(solution)/shard_map/all_to_all | solution.py:50
  22.4 0.0 copy-start.2
  22.4 0.0 collective-permute-start
  23.1 0.7 broadcast_select_fusion
  23.8 0.6 broadcast_in_dim.28
  24.4 3.9 %all-to-all-start = ((s32[16,4,128]{2,1,0:T(4,128)}), s32[16,4,128]{2,1,0:T(4,128)S(1)}, u32[]{:S(2)}, u32[]{:S(2)}) async-start(s32[16,4,128]{2,1,0:T(4,128)} %broadcast_in_dim.28), calls=%async_computation | async-start | bytes 65536 | tf_op jit(solution)/shard_map/all_to_all | solution.py:50
  28.3 0.0 copy-start.4
  28.3 0.9 copy-done.4
  29.3 0.4 shard_map.69.refs_2_
  29.6 0.0 copy-start
  29.6 1.0 copy-done
  30.6 4.3 %all-to-all-done = s32[16,4,128]{2,1,0:T(4,128)S(1)} async-done(((s32[16,4,128]{2,1,0:T(4,128)}), s32[16,4,128]{2,1,0:T(4,128)S(1)}, u32[]{:S(2)}, u32[]{:S(2)}) %all-to-all-start) | async-done | bytes 32800 | tf_op jit(solution)/shard_map/all_to_all | solution.py:50
  35.0 3.1 %shard_map.68 = (s32[16,128]{1,0:T(8,128)S(1)}, s32[1]{0:T(128)}) custom-call(s32[64,128]{1,0:T(8,128)S(1)} %bitcast.34), custom_call_target="tpu_custom_call" | custom-call | flops 10000000 | bytes 1048576 | tf_op jit(solution)/shard_map/pallas_call | solution.py:344
  38.1 0.0 collective-permute-done.refs_6_
  38.1 0.0 copy-start.5
  38.1 0.8 copy-done.5
  38.9 0.0 copy-done.2
  38.9 0.0 copy-start.1
  38.9 1.2 copy-done.1
  40.2 0.0 copy-start.3
  40.2 1.0 copy-done.3
  41.2 0.0 copy-start.6
  41.2 1.0 copy-done.6
  42.2 0.0 copy-start.7
  42.2 0.8 copy-done.7
  43.1 0.0 copy-start.8
  43.1 0.8 copy-done.8
  43.9 35.2 %shard_map.70 = (f32[14336,128]{1,0:T(8,128)S(1)}, f32[14336,128]{1,0:T(8,128)S(1)}, f32[14336,128]{1,0:T(8,128)S(1)}, f32[14336,128]{1,0:T(8,128)S(1)}, bf16[24...) custom-call(s32[2048]{0:T(1024)S(1)} %bitcast.28, ...), custom_call_target="tpu_custom_call" | custom-call | flops 100000000 | bytes 1048576 | tf_op jit(solution)/shard_map/pallas_call | solution.py:344
  79.2 12.6 %all_to_all.61 = f32[16,32,128]{2,1,0:T(8,128)S(1)} all-to-all(f32[16,32,128]{2,1,0:T(8,128)S(1)} %bitcast.22), channel_id=1, replica_groups=mesh['grp'=2,'blk'=4,'col'=2,'rep'=2] {'blk','col','rep'}, dimensions={0} | all-to-all | bytes 524288 | tf_op jit(solution)/shard_map/all_to_all | solution.py:50
  91.8 7.0 %shard_map.71 = (f32[512,128]{1,0:T(8,128)S(1)}, f32[8,128]{1,0:T(8,128)S(1)}, f32[128,128]{1,0:T(8,128)S(1)}, f32[512,128]{1,0:T(8,128)S(1)}, f32[512,128]{1,0:T(8,128)S(1)}) custom-call(s32[2048]{0:T(1024)S(1)} %bitcast.29, s32[1]{0:T(128)} %get-tuple-element.27.refs_1_, bf16[4224,128]{1,0:T(8,128)(2,1)S(1)} %copy-done.1, ...), custom_call_target="tpu_custom_call" | custom-call | flops 100000000 | bytes 1048576 | tf_op jit(solution)/shard_map/pallas_call | solution.py:344
  98.8 12.6 %all_to_all.62 = f32[16,32,128]{2,1,0:T(8,128)S(1)} all-to-all(f32[16,32,128]{2,1,0:T(8,128)S(1)} %bitcast.23), channel_id=1, replica_groups=mesh['grp'=2,'blk'=4,'col'=2,'rep'=2] {'blk','col','rep'}, dimensions={0} | all-to-all | bytes 524288 | tf_op jit(solution)/shard_map/all_to_all | solution.py:50
  111.5 7.1 %shard_map.72 = (f32[128,128]{1,0:T(8,128)S(1)}, f32[8,128]{1,0:T(8,128)S(1)}, f32[128,128]{1,0:T(8,128)S(1)}, f32[128,128]{1,0:T(8,128)S(1)}, f32[128,128]{1,0:T(8,128)S(1)}, /*index=5*/f32[128,128]{1,0:T(8,128)S(1)}) custom-call(s32[2048]{0:T(1024)S(1)} %bitcast.30, s32[1]{0:T(128)} %get-tuple-element.27.refs_1_, bf16[4224,128]{1,0:T(8,128)(2,1)S(1)} %copy-done.1, ...), custom_call_target="tpu_custom_call" | custom-call | flops 100000000 | bytes 1048576 | tf_op jit(solution)/shard_map/pallas_call | solution.py:344
  118.6 6.5 %all_to_all.63 = f32[4,32,128]{2,1,0:T(8,128)S(1)} all-to-all(f32[4,32,128]{2,1,0:T(8,128)S(1)} %bitcast.33), channel_id=1, replica_groups=mesh['grp'=2,'blk'=4,'col'=2,'rep'=2] {'col','rep'}, dimensions={0} | all-to-all | bytes 131072 | tf_op jit(solution)/shard_map/all_to_all | solution.py:50
  125.1 9.5 %all_to_all.64 = f32[16,8,128]{2,1,0:T(8,128)S(1)} all-to-all(f32[16,8,128]{2,1,0:T(8,128)S(1)} %bitcast.32), channel_id=1, replica_groups=mesh['grp'=2,'blk'=4,'col'=2,'rep'=2] {'blk','col','rep'}, dimensions={0} | all-to-all | bytes 131072 | tf_op jit(solution)/shard_map/all_to_all | solution.py:50
  134.6 0.7 shard_map.73
  (3 shorter events, 0.1 us)
Async XLA Ops:
  22.4 16.5 %copy-start.2 = (f32[4,256,128]{2,1,0:T(8,128)}, f32[4,256,128]{2,1,0:T(8,128)S(1)}, u32[]{:S(2)}) copy-start(f32[4,256,128]{2,1,0:T(8,128)S(1)} %all_to_all.60) | copy-start | bytes 1572868
  22.4 15.7 %collective-permute-start = (f32[1024,128]{1,0:T(8,128)S(1)}, f32[1024,128]{1,0:T(8,128)S(1)}, u32[]{:S(2)}, u32[]{:S(2)}) collective-permute-start(f32[1024,128]{1,0:T(8,128)S(1)} %bitcast.18), channel_id=1, source_target_pairs={{0,1},{1,0},{2,3},{3,2},{4,5},{5,4},{6,7},{7,6},{8,9},{9,8},{10,11... | collective-permute-start | bytes 1572872 | tf_op jit(solution)/shard_map/ppermute | solution.py:372
  24.4 10.5 %all-to-all-start = ((s32[16,4,128]{2,1,0:T(4,128)}), s32[16,4,128]{2,1,0:T(4,128)S(1)}, u32[]{:S(2)}, u32[]{:S(2)}) async-start(s32[16,4,128]{2,1,0:T(4,128)} %broadcast_in_dim.28), calls=%async_computation | async-start | bytes 65536 | tf_op jit(solution)/shard_map/all_to_all | solution.py:50
  28.3 1.0 copy-start.4
  29.6 1.0 copy-start
  38.1 0.8 copy-start.5
  38.9 1.2 copy-start.1
  40.2 1.0 copy-start.3
  41.2 1.0 copy-start.6
  42.2 0.8 copy-start.7
  43.1 0.8 copy-start.8
where the time goes:
time: 138 us; the launch traced here: 135 us
  blocking collectives  61.8 us (45%)
  Pallas kernels  53.6 us (39%)
  local copies, waits for them, and re-layouts  8.5 us (6%)
  waiting for transfers between devices  4.33 us (3%)
  starting transfers between devices  3.88 us (3%)
  other arithmetic  1.74 us (1%)
  between operations  1.41 us (1%)
    all_to_all x5, blocking collectives, exchange(): return lax.all_to_all(x, axes, split_axis=0, concat_axis=0, tiled=True)  61.8 us
    pallas_call x6, Pallas kernels, call(): pl.pallas_call(kernel, in_specs=in_specs, out_shape=shapes, out_specs=out...  53.6 us
    unnamed x18, local copies, waits for them, and re-layouts  7.74 us
    all_to_all x1, waiting for transfers between devices, exchange(): return lax.all_to_all(x, axes, split_axis=0, concat_axis=0, tiled=True)  4.33 us
    all_to_all x1, starting transfers between devices, exchange(): return lax.all_to_all(x, axes, split_axis=0, concat_axis=0, tiled=True)  3.88 us
  transfers between devices with their start and end apart: 2, of which 1 were waited for; matrix products, arithmetic and copies ran while one was open for 1% of the time, Pallas kernels for 3%

commit v1 on v0

--- a/solution.py
+++ b/solution.py
@@ -14,8 +14,6 @@
 UNROLL = 4
 ARRAYS = 4
 MIB = 1024 * 1024
-EVERY = ("blk", "col", "rep")
-PLANE = ("col", "rep")
 VMEM = pl.BlockSpec(memory_space=pltpu.VMEM)
 SMEM = pl.BlockSpec(memory_space=pltpu.SMEM)
 ANY = pl.BlockSpec(memory_space=pl.ANY)
@@ -46,12 +44,41 @@
         )
 
 
-def exchange(x, axes):
-    return lax.all_to_all(x, axes, split_axis=0, concat_axis=0, tiled=True)
-
-
-def copies(x, count):
-    return jnp.broadcast_to(x[None], (count,) + x.shape).reshape((count * x.shape[0],) + x.shape[1:])
+def swap(x, axis, code):
+    return lax.ppermute(x, axis, [(i, i ^ code) for i in range(lax.axis_size(axis))])
+
+
+def along_blk(x):
+    return jnp.concatenate([x] + [swap(x, "blk", k) for k in range(1, lax.axis_size("blk"))], axis=0)
+
+
+def over_plane(x):
+    reps = lax.axis_size("rep")
+    found = {0: x}
+    for c in range(1, lax.axis_size("col")):
+        found[c * reps] = swap(x, "col", c)
+    for start in sorted(found):
+        for r in range(1, reps):
+            found[start + r] = swap(found[start], "rep", r)
+    return [found[k] for k in sorted(found)]
+
+
+def assemble(sz, refs, rows, target):
+    me = sz.me()
+    for k, ref in enumerate(refs):
+        for z in range(ref.shape[0] // rows):
+            start = pl.multiple_of(jnp.bitwise_xor(me, z * sz.plane + k) * rows, 8)
+            target[pl.ds(start, rows), :] = ref[z * rows : (z + 1) * rows, :]
+
+
+def features_of(x_row, y_row, z_row, order):
+    feature = lax.broadcasted_iota(jnp.int32, (8, BS), 0)
+    x, y, z = ((row - 0.5) * (4.0 / SUPPORT) for row in (x_row, y_row, z_row))
+    factor, unit, norm = order
+    feats = jnp.where(feature == unit, 1.0, 0.0)
+    for place, row in ((0, factor * x), (1, factor * y), (2, factor * z), (norm, x * x + y * y + z * z)):
+        feats = jnp.where(feature == place, row, feats)
+    return split3(feats)
 
 
 def split3(x):
@@ -61,26 +88,26 @@
     return high, middle, rest - middle
 
 
-def lhs_kernel(sz, coords_ref, out_ref):
+def lhs_kernel(sz, home_ref, out_ref):
     quarter = lax.axis_index("col") * sz.reps + lax.axis_index("rep")
-    unit = jnp.ones((1, BS), F32)
     for i in range(sz.own):
-        start = pl.multiple_of((quarter * sz.own + i) * BS, BS)
-        x = (coords_ref[:, pl.ds(start, BS)] - 0.5) * (4.0 / SUPPORT)
-        norm = jnp.sum(x * x, axis=0, keepdims=True)
-        h, m, l = split3(jnp.concatenate([x, unit, norm, jnp.zeros((3, BS), F32)], axis=0))
+        rows = (home_ref[pl.ds(c * sz.local_blocks + quarter * sz.own + i, 1), :] for c in range(3))
+        h, m, l = features_of(*rows, (1.0, 3, 4))
         feats = jnp.concatenate([h, h, m, m, h, l, jnp.zeros((BS - DEPTH, BS), F32)], axis=0)
         out_ref[i * BS : (i + 1) * BS, :] = feats.T.astype(BF16)
     out_ref[sz.own * BS :, :] = jnp.zeros((BS, BS), BF16)
 
 
-def list_kernel(sz, pairs_ref, out_ref, count_ref, target, other, place, value, key_column, key_row, entry_row):
+def list_kernel(sz, *refs):
     me = sz.me()
+    out_ref, count_ref, target, other, place, value, key_column, key_row, entry_row = refs[sz.plane :]
     lines = sz.slots // BS
     at = 2 * lines * sz.devs
     for base in range(0, at, 2 * lines):
-        rows = pairs_ref[base : base + lines, :]
-        cols = pairs_ref[base + lines : base + 2 * lines, :]
+        pairs_ref = refs[base // (2 * lines * sz.blks)]
+        start = base % (2 * lines * sz.blks)
+        rows = pairs_ref[start : start + lines, :]
+        cols = pairs_ref[start + lines : start + 2 * lines, :]
         target[base : base + lines, :] = rows
         other[base : base + lines, :] = cols
         target[base + lines : base + 2 * lines, :] = cols
@@ -232,39 +259,35 @@
         out_ref[i : i + 1, :] = y[0:1, :] * sz.scale
 
 
-def fan_out(ref, rows, value):
-    for k in range(ref.shape[0] // rows):
-        ref[k * rows : (k + 1) * rows, :] = value
-
-
 def total_of(x):
     return jnp.sum(jnp.sum(x, axis=0, keepdims=True), axis=1, keepdims=True)
 
 
+def place_block(piece_ref, part, first, obs_ref, rhs_ref):
+    obs_ref[pl.ds(first, part), :] = piece_ref[3 * part : 4 * part, :]
+
+    def one(k, unused):
+        h, m, l = features_of(*(piece_ref[pl.ds(c * part + k, 1), :] for c in range(3)), (-2.0, 4, 3))
+        feats = jnp.concatenate([h, m, h, m, l, h], axis=0).astype(BF16)
+        rhs_ref[pl.ds(pl.multiple_of((first + k) * DEPTH, DEPTH), DEPTH), :] = feats
+        return unused
+
+    lax.fori_loop(0, part, one, 0, unroll=4)
+
+
 def first_kernel(sz, *refs):
-    list_ref, count_ref, lhs_ref, nugget_ref, obs_home_ref, near_ref, far_ref = refs[:7]
-    tile_refs = refs[7 : 7 + ARRAYS]
-    spare_ref, obs_ref, diag_ref, mapped_ref, norm_ref, rhs_ref, acc, acc_ones, total_row, done = refs[7 + ARRAYS :]
-    rep = lax.axis_index("rep")
-    part = sz.local_blocks // sz.reps
-    feature = lax.broadcasted_iota(jnp.int32, (8, BS), 0)
-    for piece_ref, turn in ((near_ref, 0), (far_ref, 1)):
-        for z in range(sz.blks):
-            base = z * 4 * part
-            first = pl.multiple_of(z * sz.local_blocks + jnp.bitwise_xor(rep, turn) * part, 8)
-            obs_ref[pl.ds(first, part), :] = piece_ref[base + 3 * part : base + 4 * part, :]
-
-            def one(k, unused, base=base, first=first, piece_ref=piece_ref):
-                x, y, z = ((piece_ref[pl.ds(base + c * part + k, 1), :] - 0.5) * (4.0 / SUPPORT) for c in range(3))
-                feats = jnp.where(feature == 4, 1.0, 0.0)
-                for place, row in enumerate((-2.0 * x, -2.0 * y, -2.0 * z, x * x + y * y + z * z)):
-                    feats = jnp.where(feature == place, row, feats)
-                h, m, l = split3(feats)
-                feats = jnp.concatenate([h, m, h, m, l, h], axis=0).astype(BF16)
-                rhs_ref[pl.ds(pl.multiple_of((first + k) * DEPTH, DEPTH), DEPTH), :] = feats
-                return unused
-
-            lax.fori_loop(0, part, one, 0, unroll=4)
+    list_ref, count_ref, lhs_ref, nugget_ref, home_ref = refs[:5]
+    coord_refs = refs[4 : 5 + (sz.blks - 1) * sz.reps]
+    refs = refs[5 + (sz.blks - 1) * sz.reps :]
+    tile_refs = refs[:ARRAYS]
+    spare_ref, obs_ref, diag_ref, mapped_ref, norm_ref, rhs_ref, acc, acc_ones, total_row, done = refs[ARRAYS:]
+    blk, rep = lax.axis_index("blk"), lax.axis_index("rep")
+    for at, piece_ref in enumerate(coord_refs[1:]):
+        code, turn = at // sz.reps + 1, at % sz.reps
+        part = sz.local_blocks // sz.reps
+        first = jnp.bitwise_xor(blk, code) * sz.local_blocks + jnp.bitwise_xor(rep, turn) * part
+        place_block(piece_ref, part, pl.multiple_of(first, 8), obs_ref, rhs_ref)
+    place_block(home_ref, sz.local_blocks, pl.multiple_of(blk * sz.local_blocks, 8), obs_ref, rhs_ref)
     count = count_ref[0]
     generate(sz, list_ref, count, lhs_ref, rhs_ref, tile_refs)
 
@@ -286,21 +309,23 @@
     own = pl.ds(pl.multiple_of(sz.me() * sz.own, 8), sz.own)
     diag = nugget_ref[pl.ds(pl.multiple_of(quarter * sz.own, 8), sz.own), :] + total_row[...]
     diag_ref[...] = diag
-    fan_out(mapped_ref, sz.own, mapped_ref[: sz.own, :] + diag * obs_ref[own, :])
+    mapped_ref[...] += diag * obs_ref[own, :]
     norm_ref[...] = jnp.broadcast_to(total_of(obs_ref[...] * obs_ref[...]), (8, BS))
 
 
 def step_kernel(sz, last, *refs):
-    list_ref, count_ref, lhs_ref, spare_ref, diag_ref, norm_ref, field_ref, resid_ref, dirn_ref, mapped = refs[:10]
-    tile_refs = refs[10 : 10 + ARRAYS]
-    rest = refs[10 + ARRAYS :]
+    list_ref, count_ref, lhs_ref, spare_ref, diag_ref, norm_ref, field_ref, resid_ref, dirn_ref = refs[:9]
+    pieces = refs[9 : 9 + sz.plane]
+    tile_refs = refs[9 + sz.plane : 9 + sz.plane + ARRAYS]
+    rest = refs[9 + sz.plane + ARRAYS :]
     mapped_ref, next_norm_ref, next_field_ref, next_resid_ref, next_dirn_ref = rest[:5]
     if last:
         dot_ref, dirn = rest[5:7]
     else:
         dirn = next_dirn_ref
-    acc, features, others, done = rest[-4:]
+    mapped, acc, features, others, done = rest[-5:]
     me = sz.me()
+    assemble(sz, pieces, sz.own, mapped)
     norm = norm_ref[0:1, 0:1]
     step = norm / total_of(dirn_ref[...] * mapped[...])
     resid = resid_ref[...] - step * mapped[...]
@@ -327,17 +352,26 @@
 
     sweep(sz, list_ref, count_ref[0], tile_refs, dirn, acc, None, remake)
     finish(sz, acc, mapped_ref)
-    ours = mapped_ref[: sz.own, :] + diag_ref[...] * dirn[own, :]
-    fan_out(mapped_ref, sz.own, ours)
+    ours = mapped_ref[...] + diag_ref[...] * dirn[own, :]
+    mapped_ref[...] = ours
     if last:
         dot_ref[...] = jnp.broadcast_to(total_of(ours * dirn[own, :]), dot_ref.shape)
 
 
-def last_kernel(sz, norm_ref, field_ref, resid_ref, dirn_ref, mapped_ref, dot_ref, out_field_ref, out_resid_ref):
-    product = jnp.sum(dot_ref[...], axis=0, keepdims=True) * 0.125
-    step = norm_ref[0:1, :] / product
+def last_kernel(sz, *refs):
+    norm_ref, field_ref, resid_ref, dirn_ref = refs[:4]
+    pieces = refs[4 : 4 + sz.plane]
+    out_field_ref, out_resid_ref = refs[4 + sz.plane :]
+    product = jnp.zeros((8, BS), F32)
+    for ref in pieces:
+        for z in range(sz.blks):
+            product = product + ref[sz.own + 8 * z : sz.own + 8 * (z + 1), :]
+    step = norm_ref[0:1, :] / product[0:1, :]
     out_field_ref[...] = field_ref[...] + step * dirn_ref[...]
-    out_resid_ref[...] = resid_ref[...] - step * mapped_ref[...]
+    quarter = lax.axis_index("col") * sz.reps + lax.axis_index("rep")
+    for k, ref in enumerate(pieces):
+        rows = pl.ds(pl.multiple_of(jnp.bitwise_xor(quarter, k) * sz.own, 8), sz.own)
+        out_resid_ref[rows, :] = resid_ref[rows, :] - step * ref[: sz.own, :]
 
 
 def call(kernel, mib, in_specs, shapes, out_specs, scratch, flops, *args):
@@ -361,15 +395,13 @@
     own, blocks, home = sz.own, sz.blocks, sz.local_blocks
     alive = jnp.arange(sz.slots, dtype=jnp.int32) < tile_live[0]
     pairs = jnp.where(alive, tile_pairs, -1).reshape(2 * sz.slots // BS, BS)
-    pairs = exchange(copies(pairs, sz.devs), EVERY)
-
     rep = lax.axis_index("rep")
-    obs_rows = observations.reshape(home, BS)
-    half = sz.points // sz.reps
-    payload = jnp.concatenate([coords, observations[None]], axis=0)
-    payload = lax.dynamic_slice_in_dim(payload, rep * half, half, axis=1)
-    near = exchange(copies(payload.reshape(4 * home // sz.reps, BS), sz.blks), "blk")
-    far = lax.ppermute(near, "rep", [(i, i ^ 1) for i in range(sz.reps)])
+    part = home // sz.reps
+    rows = jnp.concatenate([coords, observations[None]], axis=0).reshape(4, home, BS)
+    half = lax.dynamic_slice_in_dim(rows, rep * part, part, axis=1).reshape(4 * part, BS)
+    rows = rows.reshape(4 * home, BS)
+    nears = [swap(half, "blk", z) for z in range(1, sz.blks)]
+    pair_arrays = over_plane(along_blk(pairs))
 
     lhs = call(
         functools.partial(lhs_kernel, sz),
@@ -379,13 +411,13 @@
         VMEM,
         [],
         10_000_000,
-        coords,
+        rows,
     )
     lines = 2 * sz.slots // BS * sz.devs
     table, count = call(
         functools.partial(list_kernel, sz),
         12,
-        [VMEM],
+        [VMEM] * sz.plane,
         (array(sz.capacity // BS, BS, dtype=jnp.int32), array(1, dtype=jnp.int32)),
         (VMEM, SMEM),
         [pltpu.VMEM((lines, BS), jnp.int32)] * 2
@@ -393,21 +425,24 @@
         + [pltpu.VMEM((sz.capacity, BS), F32)]
         + [pltpu.VMEM((sz.capacity // BS, BS), F32)] * 2,
         10_000_000,
-        pairs,
+        *pair_arrays,
     )
-    table = table.reshape(sz.capacity)
+    table, lhs, *nears = lax.optimization_barrier((table.reshape(sz.capacity), lhs, *nears))
+    coord_arrays = []
+    for near in nears:
+        coord_arrays += [near] + [swap(near, "rep", r) for r in range(1, sz.reps)]
     tall = pltpu.VMEM(((own + 1) * BS, BS), F32)
     kept = [pltpu.VMEM((sz.kept * BS, BS), F32)] * ARRAYS
     *tiles, spare, obs, diag, mapped, norm = call(
         functools.partial(first_kernel, sz),
         sz.first_mib,
-        [SMEM, SMEM] + [VMEM] * 5,
+        [SMEM, SMEM] + [VMEM] * (3 + len(coord_arrays)),
         kept
         + [
             pltpu.HBM((blocks * DEPTH, BS), BF16),
             array(blocks, BS),
             array(own, BS),
-            array(sz.devs * own, BS),
+            array(own, BS),
             array(8, BS),
         ],
         [VMEM] * ARRAYS + [ANY] + [VMEM] * 4,
@@ -423,9 +458,8 @@
         count,
         lhs,
         nugget.reshape(home, BS),
-        obs_rows,
-        near,
-        far,
+        rows,
+        *coord_arrays,
     )
     tiles = [pltpu.with_memory_space_constraint(tile, pltpu.VMEM) for tile in tiles]
     spare = pltpu.with_memory_space_constraint(spare, pltpu.HBM)
@@ -433,15 +467,14 @@
     for sweep_index in range(1, ITERS):
         last = sweep_index + 1 == ITERS
         span = home if last else blocks
-        peers = sz.plane if last else sz.devs
-        outs = [array(peers * own, BS), array(8, BS), array(home, BS), array(span, BS), array(span, BS)]
+        outs = [array(own, BS), array(8, BS), array(home, BS), array(span, BS), array(span, BS)]
         mapped, norm, field, resid, dirn, *dot = call(
             functools.partial(step_kernel, sz, last),
             5,
-            [SMEM, SMEM, ANY, ANY] + [VMEM] * (6 + ARRAYS),
-            outs + [array(8 * sz.devs, BS)] * last,
+            [SMEM, SMEM, ANY, ANY] + [VMEM] * (5 + sz.plane + ARRAYS),
+            outs + [array(8, BS)] * last,
             [VMEM] * (len(outs) + last),
-            [pltpu.VMEM((blocks, BS), F32)] * last
+            [pltpu.VMEM((blocks, BS), F32)] * (1 + last)
             + [tall, pltpu.VMEM((BS, BS), BF16), pltpu.VMEM((DEPTH, BS), BF16), pltpu.SemaphoreType.DMA],
             100_000_000,
             table,
@@ -453,13 +486,14 @@
             field,
             resid,
             dirn,
-            exchange(mapped, EVERY),
+            *over_plane(along_blk(mapped)),
             *tiles,
         )
+    ends = over_plane(jnp.concatenate([mapped, along_blk(dot[0])], axis=0))
     field, resid = call(
         functools.partial(last_kernel, sz),
         4,
-        [VMEM] * 6,
+        [VMEM] * (4 + sz.plane),
         (array(home, BS), array(home, BS)),
         (VMEM, VMEM),
         [],
@@ -468,8 +502,7 @@
         field,
         resid,
         dirn,
-        exchange(mapped, PLANE),
-        exchange(dot[0], EVERY),
+        *ends,
     )
     return field.reshape(sz.points), resid.reshape(sz.points)
 

time: 138 us -> 118 us (0.86)
  the two profiles are of different devices: /device:TPU:0 before, /device:TPU:13 now
where the time goes in v1:
time: 118 us; the launch traced here: 116 us
  Pallas kernels  49.1 us (42%)
  starting transfers between devices  44 us (37%)
  waiting for transfers between devices  15.6 us (13%)
  local copies, waits for them, and re-layouts  3.58 us (3%)
  other arithmetic  2.58 us (2%)
  between operations  1.47 us (1%)
    pallas_call x6, Pallas kernels, call(): pl.pallas_call(kernel, in_specs=in_specs, out_shape=shapes, out_specs=out...  49.1 us
    ppermute x30, starting transfers between devices, swap(): lax.ppermute(x, axis, [(i, i ^ code) for i in range(lax.axis_size(axis))])  44 us
    ppermute x30, waiting for transfers between devices, swap(): lax.ppermute(x, axis, [(i, i ^ code) for i in range(lax.axis_size(axis))])  15.6 us
    unnamed x17, local copies, waits for them, and re-layouts  3.37 us
  transfers between devices with their start and end apart: 30, of which 13 were waited for; matrix products, arithmetic and copies ran while one was open for 3% of the time, Pallas kernels for 3%

profile of v1, /device:TPU:13, one launch (start us, length us, event | category | flops | bytes accessed | tf_op | source)
XLA Modules:
  0.0 116.3 jit_solution(15363779946927514166)
XLA Ops:
  1.3 0.7 broadcast_select_fusion
  2.0 1.3 %collective-permute-start.2 = (s32[4,128]{1,0:T(4,128)S(1)}, s32[4,128]{1,0:T(4,128)S(1)}, u32[]{:S(2)}, u32[]{:S(2)}) collective-permute-start(s32[4,128]{1,0:T(4,128)S(1)} %reshape.26), channel_id=1, source_target_pairs={{0,12},{4,8},{8,4},{12,0},{1,13},{5,9},{9,5},{13,1},{2,14},{6,10},... | collective-permute-start | bytes 6152 | tf_op jit(solution)/shard_map/ppermute | solution.py:48
  3.3 1.1 collective-permute-start.1
  4.4 1.1 collective-permute-start
  5.5 1.0 copy.9
  6.5 0.2 collective-permute-done.1
  6.6 0.2 collective-permute-done
  6.8 1.3 %collective-permute-start.4 = (s32[16,128]{1,0:T(8,128)S(1)}, s32[16,128]{1,0:T(8,128)S(1)}, u32[]{:S(2)}, u32[]{:S(2)}) collective-permute-start(s32[16,128]{1,0:T(8,128)S(1)} %pad_add_fusion.refs_0_), channel_id=1, source_target_pairs={{0,2},{2,0},{1,3},{3,1},{4,6},{6,4},{5,7},{7,5},{8,10},{10,8},{9,1... | collective-permute-start | bytes 24584 | tf_op jit(solution)/shard_map/ppermute | solution.py:48
  8.1 0.8 fusion
  8.9 2.4 %collective-permute-start.8 = (f32[256,128]{1,0:T(8,128)S(1)}, f32[256,128]{1,0:T(8,128)S(1)}, u32[]{:S(2)}, u32[]{:S(2)}) collective-permute-start(f32[256,128]{1,0:T(8,128)S(1)} %bitcast.21), channel_id=1, source_target_pairs={{0,12},{4,8},{8,4},{12,0},{1,13},{5,9},{9,5},{13,1},{2,14},{6,10},... | collective-permute-start | bytes 393224 | tf_op jit(solution)/shard_map/ppermute | solution.py:48
  11.2 1.8 %collective-permute-start.7 = (f32[256,128]{1,0:T(8,128)S(1)}, f32[256,128]{1,0:T(8,128)S(1)}, u32[]{:S(2)}, u32[]{:S(2)}) collective-permute-start(f32[256,128]{1,0:T(8,128)S(1)} %bitcast.22), channel_id=1, source_target_pairs={{0,8},{4,12},{8,0},{12,4},{1,9},{5,13},{9,1},{13,5},{2,10},{6,14},... | collective-permute-start | bytes 393224 | tf_op jit(solution)/shard_map/ppermute | solution.py:48
  13.0 2.9 %collective-permute-start.3 = (s32[16,128]{1,0:T(8,128)S(1)}, s32[16,128]{1,0:T(8,128)S(1)}, u32[]{:S(2)}, u32[]{:S(2)}) collective-permute-start(s32[16,128]{1,0:T(8,128)S(1)} %pad_add_fusion.refs_0_), channel_id=1, source_target_pairs={{0,1},{1,0},{2,3},{3,2},{4,5},{5,4},{6,7},{7,6},{8,9},{9,8},{10,11... | collective-permute-start | bytes 24584 | tf_op jit(solution)/shard_map/ppermute | solution.py:48
  16.1 1.1 pad_maximum_fusion
  17.2 0.2 reshape_reshape.3.home_ref.refs_4_
  17.4 0.4 shard_map.69.refs_2_
  17.7 3.1 %shard_map.68 = (s32[16,128]{1,0:T(8,128)S(1)}, s32[1]{0:T(128)}) custom-call(s32[16,128]{1,0:T(8,128)S(1)} %pad_add_fusion.refs_0_, s32[16,128]{1,0:T(8,128)S(1)} %collective-permute-done.3.refs_1_, s32[16,128]{1,0:T(8,128)S(1)} %collective-permute-done.4.refs_2_, s32[16,128]{1,0:T(8,128)S(1)} %collective-permute-done.5.refs_3_), custom_call_target="tpu_custom_call" | custom-call | flops 10000000 | bytes 1048576 | tf_op jit(solution)/shard_map/pallas_call | solution.py:378
  20.9 1.0 collective-permute-done.7.refs_7_
  21.9 1.5 %collective-permute-start.9 = (f32[256,128]{1,0:T(8,128)S(1)}, f32[256,128]{1,0:T(8,128)S(1)}, u32[]{:S(2)}, u32[]{:S(2)}) collective-permute-start(f32[256,128]{1,0:T(8,128)S(1)} %collective-permute-done.6.refs_5_), channel_id=1, source_target_pairs={{0,1},{1,0},{2,3},{3,2},{4,5},{5,4},{6,7},{7,6},{8,9},{9,8},{10,11... | collective-permute-start | bytes 393224 | tf_op jit(solution)/shard_map/ppermute | solution.py:48
  23.4 0.6 copy-done
  24.0 0.5 collective-permute-start.11
  24.5 0.8 collective-permute-done.10.refs_8_
  25.4 0.2 collective-permute-done.11.refs_10_
  25.5 0.9 copy-done.1
  26.5 0.8 copy-done.2
  27.3 31.7 %shard_map.70 = (f32[14336,128]{1,0:T(8,128)S(1)}, f32[14336,128]{1,0:T(8,128)S(1)}, f32[14336,128]{1,0:T(8,128)S(1)}, f32[14336,128]{1,0:T(8,128)S(1)}, bf16[24...) custom-call(s32[2048]{0:T(1024)S(1)} %bitcast.13, ...), custom_call_target="tpu_custom_call" | custom-call | flops 100000000 | bytes 1048576 | tf_op jit(solution)/shard_map/pallas_call | solution.py:378
  59.1 11.2 %collective-permute-start.13 = (f32[32,128]{1,0:T(8,128)S(1)}, f32[32,128]{1,0:T(8,128)S(1)}, u32[]{:S(2)}, u32[]{:S(2)}) collective-permute-start(f32[32,128]{1,0:T(8,128)S(1)} %get-tuple-element.42), channel_id=1, source_target_pairs={{0,8},{4,12},{8,0},{12,4},{1,9},{5,13},{9,1},{13,5},{2,10},{6,14},... | collective-permute-start | bytes 49160 | tf_op jit(solution)/shard_map/ppermute | solution.py:48
  70.3 2.6 %collective-permute-done.12 = f32[32,128]{1,0:T(8,128)S(1)} collective-permute-done((f32[32,128]{1,0:T(8,128)S(1)}, f32[32,128]{1,0:T(8,128)S(1)}, u32[]{:S(2)}, u32[]{:S(2)}) %collective-permute-start.12) | collective-permute-done | bytes 16416 | tf_op jit(solution)/shard_map/ppermute | solution.py:48
  72.9 0.6 collective-permute-start.16
  73.5 2.8 %collective-permute-done.16.refs_11_ = f32[128,128]{1,0:T(8,128)S(1)} collective-permute-done((f32[128,128]{1,0:T(8,128)S(1)}, f32[128,128]{1,0:T(8,128)S(1)}, u32[]{:S(2)}, u32[]{:S(2)}) %collective-permute-start.16) | collective-permute-done | bytes 65568 | tf_op jit(solution)/shard_map/ppermute | solution.py:48
  76.3 0.3 collective-permute-start.17
  76.6 0.9 collective-permute-done.17.refs_12_
  77.6 6.5 %shard_map.71 = (f32[32,128]{1,0:T(8,128)S(1)}, f32[8,128]{1,0:T(8,128)S(1)}, f32[128,128]{1,0:T(8,128)S(1)}, f32[512,128]{1,0:T(8,128)S(1)}, f32[512,128]{1,0:T(8,128)S(1)}) custom-call(s32[2048]{0:T(1024)S(1)} %bitcast.14, s32[1]{0:T(128)} %get-tuple-element.33.refs_1_, bf16[4224,128]{1,0:T(8,128)(2,1)S(1)} %shard_map.69.refs_2_, ...), custom_call_target="tpu_custom_call" | custom-call | flops 100000000 | bytes 1048576 | tf_op jit(solution)/shard_map/pallas_call | solution.py:378
  84.2 2.8 %collective-permute-start.19 = (f32[32,128]{1,0:T(8,128)S(1)}, f32[32,128]{1,0:T(8,128)S(1)}, u32[]{:S(2)}, u32[]{:S(2)}) collective-permute-start(f32[32,128]{1,0:T(8,128)S(1)} %get-tuple-element.51), channel_id=1, source_target_pairs={{0,8},{4,12},{8,0},{12,4},{1,9},{5,13},{9,1},{13,5},{2,10},{6,14},... | collective-permute-start | bytes 49160 | tf_op jit(solution)/shard_map/ppermute | solution.py:48
  87.0 2.6 %collective-permute-done.18 = f32[32,128]{1,0:T(8,128)S(1)} collective-permute-done((f32[32,128]{1,0:T(8,128)S(1)}, f32[32,128]{1,0:T(8,128)S(1)}, u32[]{:S(2)}, u32[]{:S(2)}) %collective-permute-start.18) | collective-permute-done | bytes 16416 | tf_op jit(solution)/shard_map/ppermute | solution.py:48
  89.7 1.1 collective-permute-start.22
  90.8 2.0 %collective-permute-start.21 = (f32[128,128]{1,0:T(8,128)S(1)}, f32[128,128]{1,0:T(8,128)S(1)}, u32[]{:S(2)}, u32[]{:S(2)}) collective-permute-start(f32[128,128]{1,0:T(8,128)S(1)} %constant_dynamic-update-slice_fusion.4.refs_9_), channel_id=1, source_target_pairs={{0,1},{1,0},{2,3},{3,2},{4,5},{5,4},{6,7},{7,6},{8,9},{9,8},{10,11... | collective-permute-start | bytes 196616 | tf_op jit(solution)/shard_map/ppermute | solution.py:48
  92.7 0.1 collective-permute-done.22.refs_11_
  92.8 2.6 %collective-permute-start.23 = (f32[128,128]{1,0:T(8,128)S(1)}, f32[128,128]{1,0:T(8,128)S(1)}, u32[]{:S(2)}, u32[]{:S(2)}) collective-permute-start(f32[128,128]{1,0:T(8,128)S(1)} %collective-permute-done.22.refs_11_), channel_id=1, source_target_pairs={{0,1},{1,0},{2,3},{3,2},{4,5},{5,4},{6,7},{7,6},{8,9},{9,8},{10,11... | collective-permute-start | bytes 196616 | tf_op jit(solution)/shard_map/ppermute | solution.py:48
  95.4 0.9 collective-permute-done.23.refs_12_
  96.3 6.6 %shard_map.72 = (f32[32,128]{1,0:T(8,128)S(1)}, f32[8,128]{1,0:T(8,128)S(1)}, f32[128,128]{1,0:T(8,128)S(1)}, f32[128,128]{1,0:T(8,128)S(1)}, f32[128,128]{1,0:T(8,128)S(1)}, /*index=5*/f32[8,128]{1,0:T(8,128)S(1)}) custom-call(s32[2048]{0:T(1024)S(1)} %bitcast.15, s32[1]{0:T(128)} %get-tuple-element.33.refs_1_, bf16[4224,128]{1,0:T(8,128)(2,1)S(1)} %shard_map.69.refs_2_, ...), custom_call_target="tpu_custom_call" | custom-call | flops 100000000 | bytes 1048576 | tf_op jit(solution)/shard_map/pallas_call | solution.py:378
  103.0 0.7 collective-permute-start.26
  103.7 3.0 %collective-permute-start.25 = (f32[8,128]{1,0:T(8,128)S(1)}, f32[8,128]{1,0:T(8,128)S(1)}, u32[]{:S(2)}, u32[]{:S(2)}) collective-permute-start(f32[8,128]{1,0:T(8,128)S(1)} %get-tuple-element.57), channel_id=1, source_target_pairs={{0,8},{4,12},{8,0},{12,4},{1,9},{5,13},{9,1},{13,5},{2,10},{6,14},... | collective-permute-start | bytes 12296 | tf_op jit(solution)/shard_map/ppermute | solution.py:48
  106.7 2.5 %collective-permute-done.24 = f32[8,128]{1,0:T(8,128)S(1)} collective-permute-done((f32[8,128]{1,0:T(8,128)S(1)}, f32[8,128]{1,0:T(8,128)S(1)}, u32[]{:S(2)}, u32[]{:S(2)}) %collective-permute-start.24) | collective-permute-done | bytes 4128 | tf_op jit(solution)/shard_map/ppermute | solution.py:48
  109.2 1.4 %collective-permute-start.28 = (f32[64,128]{1,0:T(8,128)S(1)}, f32[64,128]{1,0:T(8,128)S(1)}, u32[]{:S(2)}, u32[]{:S(2)}) collective-permute-start(f32[64,128]{1,0:T(8,128)S(1)} %constant_dynamic-update-slice_fusion.8.refs_4_), channel_id=1, source_target_pairs={{0,2},{2,0},{1,3},{3,1},{4,6},{6,4},{5,7},{7,5},{8,10},{10,8},{9,1... | collective-permute-start | bytes 98312 | tf_op jit(solution)/shard_map/ppermute | solution.py:48
  110.5 2.0 %collective-permute-start.27 = (f32[64,128]{1,0:T(8,128)S(1)}, f32[64,128]{1,0:T(8,128)S(1)}, u32[]{:S(2)}, u32[]{:S(2)}) collective-permute-start(f32[64,128]{1,0:T(8,128)S(1)} %constant_dynamic-update-slice_fusion.8.refs_4_), channel_id=1, source_target_pairs={{0,1},{1,0},{2,3},{3,2},{4,5},{5,4},{6,7},{7,6},{8,9},{9,8},{10,11... | collective-permute-start | bytes 98312 | tf_op jit(solution)/shard_map/ppermute | solution.py:48
  112.5 2.3 %collective-permute-start.29 = (f32[64,128]{1,0:T(8,128)S(1)}, f32[64,128]{1,0:T(8,128)S(1)}, u32[]{:S(2)}, u32[]{:S(2)}) collective-permute-start(f32[64,128]{1,0:T(8,128)S(1)} %collective-permute-done.28.refs_6_), channel_id=1, source_target_pairs={{0,1},{1,0},{2,3},{3,2},{4,5},{5,4},{6,7},{7,6},{8,9},{9,8},{10,11... | collective-permute-start | bytes 98312 | tf_op jit(solution)/shard_map/ppermute | solution.py:48
  114.8 0.9 collective-permute-done.29.refs_7_
  115.7 0.7 shard_map.73
  (45 shorter events, 0.3 us)
Async XLA Ops:
  2.0 4.5 %collective-permute-start.2 = (s32[4,128]{1,0:T(4,128)S(1)}, s32[4,128]{1,0:T(4,128)S(1)}, u32[]{:S(2)}, u32[]{:S(2)}) collective-permute-start(s32[4,128]{1,0:T(4,128)S(1)} %reshape.26), channel_id=1, source_target_pairs={{0,12},{4,8},{8,4},{12,0},{1,13},{5,9},{9,5},{13,1},{2,14},{6,10},... | collective-permute-start | bytes 6152 | tf_op jit(solution)/shard_map/ppermute | solution.py:48
  3.3 3.3 %collective-permute-start.1 = (s32[4,128]{1,0:T(4,128)S(1)}, s32[4,128]{1,0:T(4,128)S(1)}, u32[]{:S(2)}, u32[]{:S(2)}) collective-permute-start(s32[4,128]{1,0:T(4,128)S(1)} %reshape.26), channel_id=1, source_target_pairs={{0,8},{4,12},{8,0},{12,4},{1,9},{5,13},{9,1},{13,5},{2,10},{6,14},... | collective-permute-start | bytes 6152 | tf_op jit(solution)/shard_map/ppermute | solution.py:48
  4.4 2.4 %collective-permute-start = (s32[4,128]{1,0:T(4,128)S(1)}, s32[4,128]{1,0:T(4,128)S(1)}, u32[]{:S(2)}, u32[]{:S(2)}) collective-permute-start(s32[4,128]{1,0:T(4,128)S(1)} %reshape.26), channel_id=1, source_target_pairs={{0,4},{4,0},{8,12},{12,8},{1,5},{5,1},{9,13},{13,9},{2,6},{6,2},{1... | collective-permute-start | bytes 6152 | tf_op jit(solution)/shard_map/ppermute | solution.py:48
  6.8 9.2 %collective-permute-start.4 = (s32[16,128]{1,0:T(8,128)S(1)}, s32[16,128]{1,0:T(8,128)S(1)}, u32[]{:S(2)}, u32[]{:S(2)}) collective-permute-start(s32[16,128]{1,0:T(8,128)S(1)} %pad_add_fusion.refs_0_), channel_id=1, source_target_pairs={{0,2},{2,0},{1,3},{3,1},{4,6},{6,4},{5,7},{7,5},{8,10},{10,8},{9,1... | collective-permute-start | bytes 24584 | tf_op jit(solution)/shard_map/ppermute | solution.py:48
  8.9 12.0 %collective-permute-start.8 = (f32[256,128]{1,0:T(8,128)S(1)}, f32[256,128]{1,0:T(8,128)S(1)}, u32[]{:S(2)}, u32[]{:S(2)}) collective-permute-start(f32[256,128]{1,0:T(8,128)S(1)} %bitcast.21), channel_id=1, source_target_pairs={{0,12},{4,8},{8,4},{12,0},{1,13},{5,9},{9,5},{13,1},{2,14},{6,10},... | collective-permute-start | bytes 393224 | tf_op jit(solution)/shard_map/ppermute | solution.py:48
  11.2 10.7 %collective-permute-start.7 = (f32[256,128]{1,0:T(8,128)S(1)}, f32[256,128]{1,0:T(8,128)S(1)}, u32[]{:S(2)}, u32[]{:S(2)}) collective-permute-start(f32[256,128]{1,0:T(8,128)S(1)} %bitcast.22), channel_id=1, source_target_pairs={{0,8},{4,12},{8,0},{12,4},{1,9},{5,13},{9,1},{13,5},{2,10},{6,14},... | collective-permute-start | bytes 393224 | tf_op jit(solution)/shard_map/ppermute | solution.py:48
  13.0 8.9 %collective-permute-start.6 = (f32[256,128]{1,0:T(8,128)S(1)}, f32[256,128]{1,0:T(8,128)S(1)}, u32[]{:S(2)}, u32[]{:S(2)}) collective-permute-start(f32[256,128]{1,0:T(8,128)S(1)} %bitcast.23), channel_id=1, source_target_pairs={{0,4},{4,0},{8,12},{12,8},{1,5},{5,1},{9,13},{13,9},{2,6},{6,2},{1... | collective-permute-start | bytes 393224 | tf_op jit(solution)/shard_map/ppermute | solution.py:48
  13.0 4.7 %collective-permute-start.3 = (s32[16,128]{1,0:T(8,128)S(1)}, s32[16,128]{1,0:T(8,128)S(1)}, u32[]{:S(2)}, u32[]{:S(2)}) collective-permute-start(s32[16,128]{1,0:T(8,128)S(1)} %pad_add_fusion.refs_0_), channel_id=1, source_target_pairs={{0,1},{1,0},{2,3},{3,2},{4,5},{5,4},{6,7},{7,6},{8,9},{9,8},{10,11... | collective-permute-start | bytes 24584 | tf_op jit(solution)/shard_map/ppermute | solution.py:48
  16.0 1.8 %collective-permute-start.5 = (s32[16,128]{1,0:T(8,128)S(1)}, s32[16,128]{1,0:T(8,128)S(1)}, u32[]{:S(2)}, u32[]{:S(2)}) collective-permute-start(s32[16,128]{1,0:T(8,128)S(1)} %collective-permute-done.4.refs_2_), channel_id=1, source_target_pairs={{0,1},{1,0},{2,3},{3,2},{4,5},{5,4},{6,7},{7,6},{8,9},{9,8},{10,11... | collective-permute-start | bytes 24584 | tf_op jit(solution)/shard_map/ppermute | solution.py:48
  21.9 2.6 %collective-permute-start.9 = (f32[256,128]{1,0:T(8,128)S(1)}, f32[256,128]{1,0:T(8,128)S(1)}, u32[]{:S(2)}, u32[]{:S(2)}) collective-permute-start(f32[256,128]{1,0:T(8,128)S(1)} %collective-permute-done.6.refs_5_), channel_id=1, source_target_pairs={{0,1},{1,0},{2,3},{3,2},{4,5},{5,4},{6,7},{7,6},{8,9},{9,8},{10,11... | collective-permute-start | bytes 393224 | tf_op jit(solution)/shard_map/ppermute | solution.py:48
  23.4 0.6 copy-start
  24.0 1.3 %collective-permute-start.10 = (f32[256,128]{1,0:T(8,128)S(1)}, f32[256,128]{1,0:T(8,128)S(1)}, u32[]{:S(2)}, u32[]{:S(2)}) collective-permute-start(f32[256,128]{1,0:T(8,128)S(1)} %collective-permute-done.7.refs_7_), channel_id=1, source_target_pairs={{0,1},{1,0},{2,3},{3,2},{4,5},{5,4},{6,7},{7,6},{8,9},{9,8},{10,11... | collective-permute-start | bytes 393224 | tf_op jit(solution)/shard_map/ppermute | solution.py:48
  24.0 1.5 %collective-permute-start.11 = (f32[256,128]{1,0:T(8,128)S(1)}, f32[256,128]{1,0:T(8,128)S(1)}, u32[]{:S(2)}, u32[]{:S(2)}) collective-permute-start(f32[256,128]{1,0:T(8,128)S(1)} %collective-permute-done.8.refs_9_), channel_id=1, source_target_pairs={{0,1},{1,0},{2,3},{3,2},{4,5},{5,4},{6,7},{7,6},{8,9},{9,8},{10,11... | collective-permute-start | bytes 393224 | tf_op jit(solution)/shard_map/ppermute | solution.py:48
  25.5 0.9 copy-start.1
  26.5 0.8 copy-start.2
  59.0 13.8 %collective-permute-start.14 = (f32[32,128]{1,0:T(8,128)S(1)}, f32[32,128]{1,0:T(8,128)S(1)}, u32[]{:S(2)}, u32[]{:S(2)}) collective-permute-start(f32[32,128]{1,0:T(8,128)S(1)} %get-tuple-element.42), channel_id=1, source_target_pairs={{0,12},{4,8},{8,4},{12,0},{1,13},{5,9},{9,5},{13,1},{2,14},{6,10},... | collective-permute-start | bytes 49160 | tf_op jit(solution)/shard_map/ppermute | solution.py:48
  59.1 13.8 %collective-permute-start.13 = (f32[32,128]{1,0:T(8,128)S(1)}, f32[32,128]{1,0:T(8,128)S(1)}, u32[]{:S(2)}, u32[]{:S(2)}) collective-permute-start(f32[32,128]{1,0:T(8,128)S(1)} %get-tuple-element.42), channel_id=1, source_target_pairs={{0,8},{4,12},{8,0},{12,4},{1,9},{5,13},{9,1},{13,5},{2,10},{6,14},... | collective-permute-start | bytes 49160 | tf_op jit(solution)/shard_map/ppermute | solution.py:48
  70.3 2.6 %collective-permute-start.12 = (f32[32,128]{1,0:T(8,128)S(1)}, f32[32,128]{1,0:T(8,128)S(1)}, u32[]{:S(2)}, u32[]{:S(2)}) collective-permute-start(f32[32,128]{1,0:T(8,128)S(1)} %get-tuple-element.42), channel_id=1, source_target_pairs={{0,4},{4,0},{8,12},{12,8},{1,5},{5,1},{9,13},{13,9},{2,6},{6,2},{1... | collective-permute-start | bytes 49160 | tf_op jit(solution)/shard_map/ppermute | solution.py:48
  72.9 3.4 %collective-permute-start.16 = (f32[128,128]{1,0:T(8,128)S(1)}, f32[128,128]{1,0:T(8,128)S(1)}, u32[]{:S(2)}, u32[]{:S(2)}) collective-permute-start(f32[128,128]{1,0:T(8,128)S(1)} %constant_dynamic-update-slice_fusion.refs_9_), channel_id=1, source_target_pairs={{0,2},{2,0},{1,3},{3,1},{4,6},{6,4},{5,7},{7,5},{8,10},{10,8},{9,1... | collective-permute-start | bytes 196616 | tf_op jit(solution)/shard_map/ppermute | solution.py:48
  73.5 3.1 %collective-permute-start.15 = (f32[128,128]{1,0:T(8,128)S(1)}, f32[128,128]{1,0:T(8,128)S(1)}, u32[]{:S(2)}, u32[]{:S(2)}) collective-permute-start(f32[128,128]{1,0:T(8,128)S(1)} %constant_dynamic-update-slice_fusion.refs_9_), channel_id=1, source_target_pairs={{0,1},{1,0},{2,3},{3,2},{4,5},{5,4},{6,7},{7,6},{8,9},{9,8},{10,11... | collective-permute-start | bytes 196616 | tf_op jit(solution)/shard_map/ppermute | solution.py:48
  76.3 1.3 %collective-permute-start.17 = (f32[128,128]{1,0:T(8,128)S(1)}, f32[128,128]{1,0:T(8,128)S(1)}, u32[]{:S(2)}, u32[]{:S(2)}) collective-permute-start(f32[128,128]{1,0:T(8,128)S(1)} %collective-permute-done.16.refs_11_), channel_id=1, source_target_pairs={{0,1},{1,0},{2,3},{3,2},{4,5},{5,4},{6,7},{7,6},{8,9},{9,8},{10,11... | collective-permute-start | bytes 196616 | tf_op jit(solution)/shard_map/ppermute | solution.py:48
  84.1 5.5 %collective-permute-start.20 = (f32[32,128]{1,0:T(8,128)S(1)}, f32[32,128]{1,0:T(8,128)S(1)}, u32[]{:S(2)}, u32[]{:S(2)}) collective-permute-start(f32[32,128]{1,0:T(8,128)S(1)} %get-tuple-element.51), channel_id=1, source_target_pairs={{0,12},{4,8},{8,4},{12,0},{1,13},{5,9},{9,5},{13,1},{2,14},{6,10},... | collective-permute-start | bytes 49160 | tf_op jit(solution)/shard_map/ppermute | solution.py:48
  84.2 5.4 %collective-permute-start.19 = (f32[32,128]{1,0:T(8,128)S(1)}, f32[32,128]{1,0:T(8,128)S(1)}, u32[]{:S(2)}, u32[]{:S(2)}) collective-permute-start(f32[32,128]{1,0:T(8,128)S(1)} %get-tuple-element.51), channel_id=1, source_target_pairs={{0,8},{4,12},{8,0},{12,4},{1,9},{5,13},{9,1},{13,5},{2,10},{6,14},... | collective-permute-start | bytes 49160 | tf_op jit(solution)/shard_map/ppermute | solution.py:48
  87.0 2.6 %collective-permute-start.18 = (f32[32,128]{1,0:T(8,128)S(1)}, f32[32,128]{1,0:T(8,128)S(1)}, u32[]{:S(2)}, u32[]{:S(2)}) collective-permute-start(f32[32,128]{1,0:T(8,128)S(1)} %get-tuple-element.51), channel_id=1, source_target_pairs={{0,4},{4,0},{8,12},{12,8},{1,5},{5,1},{9,13},{13,9},{2,6},{6,2},{1... | collective-permute-start | bytes 49160 | tf_op jit(solution)/shard_map/ppermute | solution.py:48
  89.7 3.2 %collective-permute-start.22 = (f32[128,128]{1,0:T(8,128)S(1)}, f32[128,128]{1,0:T(8,128)S(1)}, u32[]{:S(2)}, u32[]{:S(2)}) collective-permute-start(f32[128,128]{1,0:T(8,128)S(1)} %constant_dynamic-update-slice_fusion.4.refs_9_), channel_id=1, source_target_pairs={{0,2},{2,0},{1,3},{3,1},{4,6},{6,4},{5,7},{7,5},{8,10},{10,8},{9,1... | collective-permute-start | bytes 196616 | tf_op jit(solution)/shard_map/ppermute | solution.py:48
  90.8 4.7 %collective-permute-start.21 = (f32[128,128]{1,0:T(8,128)S(1)}, f32[128,128]{1,0:T(8,128)S(1)}, u32[]{:S(2)}, u32[]{:S(2)}) collective-permute-start(f32[128,128]{1,0:T(8,128)S(1)} %constant_dynamic-update-slice_fusion.4.refs_9_), channel_id=1, source_target_pairs={{0,1},{1,0},{2,3},{3,2},{4,5},{5,4},{6,7},{7,6},{8,9},{9,8},{10,11... | collective-permute-start | bytes 196616 | tf_op jit(solution)/shard_map/ppermute | solution.py:48
  92.8 3.5 %collective-permute-start.23 = (f32[128,128]{1,0:T(8,128)S(1)}, f32[128,128]{1,0:T(8,128)S(1)}, u32[]{:S(2)}, u32[]{:S(2)}) collective-permute-start(f32[128,128]{1,0:T(8,128)S(1)} %collective-permute-done.22.refs_11_), channel_id=1, source_target_pairs={{0,1},{1,0},{2,3},{3,2},{4,5},{5,4},{6,7},{7,6},{8,9},{9,8},{10,11... | collective-permute-start | bytes 196616 | tf_op jit(solution)/shard_map/ppermute | solution.py:48
  103.0 6.2 %collective-permute-start.26 = (f32[8,128]{1,0:T(8,128)S(1)}, f32[8,128]{1,0:T(8,128)S(1)}, u32[]{:S(2)}, u32[]{:S(2)}) collective-permute-start(f32[8,128]{1,0:T(8,128)S(1)} %get-tuple-element.57), channel_id=1, source_target_pairs={{0,12},{4,8},{8,4},{12,0},{1,13},{5,9},{9,5},{13,1},{2,14},{6,10},... | collective-permute-start | bytes 12296 | tf_op jit(solution)/shard_map/ppermute | solution.py:48
  103.7 5.5 %collective-permute-start.25 = (f32[8,128]{1,0:T(8,128)S(1)}, f32[8,128]{1,0:T(8,128)S(1)}, u32[]{:S(2)}, u32[]{:S(2)}) collective-permute-start(f32[8,128]{1,0:T(8,128)S(1)} %get-tuple-element.57), channel_id=1, source_target_pairs={{0,8},{4,12},{8,0},{12,4},{1,9},{5,13},{9,1},{13,5},{2,10},{6,14},... | collective-permute-start | bytes 12296 | tf_op jit(solution)/shard_map/ppermute | solution.py:48
  106.7 2.5 %collective-permute-start.24 = (f32[8,128]{1,0:T(8,128)S(1)}, f32[8,128]{1,0:T(8,128)S(1)}, u32[]{:S(2)}, u32[]{:S(2)}) collective-permute-start(f32[8,128]{1,0:T(8,128)S(1)} %get-tuple-element.57), channel_id=1, source_target_pairs={{0,4},{4,0},{8,12},{12,8},{1,5},{5,1},{9,13},{13,9},{2,6},{6,2},{1... | collective-permute-start | bytes 12296 | tf_op jit(solution)/shard_map/ppermute | solution.py:48
  109.2 3.3 %collective-permute-start.28 = (f32[64,128]{1,0:T(8,128)S(1)}, f32[64,128]{1,0:T(8,128)S(1)}, u32[]{:S(2)}, u32[]{:S(2)}) collective-permute-start(f32[64,128]{1,0:T(8,128)S(1)} %constant_dynamic-update-slice_fusion.8.refs_4_), channel_id=1, source_target_pairs={{0,2},{2,0},{1,3},{3,1},{4,6},{6,4},{5,7},{7,5},{8,10},{10,8},{9,1... | collective-permute-start | bytes 98312 | tf_op jit(solution)/shard_map/ppermute | solution.py:48
  110.5 4.3 %collective-permute-start.27 = (f32[64,128]{1,0:T(8,128)S(1)}, f32[64,128]{1,0:T(8,128)S(1)}, u32[]{:S(2)}, u32[]{:S(2)}) collective-permute-start(f32[64,128]{1,0:T(8,128)S(1)} %constant_dynamic-update-slice_fusion.8.refs_4_), channel_id=1, source_target_pairs={{0,1},{1,0},{2,3},{3,2},{4,5},{5,4},{6,7},{7,6},{8,9},{9,8},{10,11... | collective-permute-start | bytes 98312 | tf_op jit(solution)/shard_map/ppermute | solution.py:48
  112.5 3.1 %collective-permute-start.29 = (f32[64,128]{1,0:T(8,128)S(1)}, f32[64,128]{1,0:T(8,128)S(1)}, u32[]{:S(2)}, u32[]{:S(2)}) collective-permute-start(f32[64,128]{1,0:T(8,128)S(1)} %collective-permute-done.28.refs_6_), channel_id=1, source_target_pairs={{0,1},{1,0},{2,3},{3,2},{4,5},{5,4},{6,7},{7,6},{8,9},{9,8},{10,11... | collective-permute-start | bytes 98312 | tf_op jit(solution)/shard_map/ppermute | solution.py:48

commit v2 on v1

--- a/solution.py
+++ b/solution.py
@@ -88,10 +88,14 @@
     return high, middle, rest - middle
 
 
+def block_row(ref, c, part, k):
+    return ref[c, pl.ds(k, 1), :] if len(ref.shape) == 3 else ref[pl.ds(c * part + k, 1), :]
+
+
 def lhs_kernel(sz, home_ref, out_ref):
     quarter = lax.axis_index("col") * sz.reps + lax.axis_index("rep")
     for i in range(sz.own):
-        rows = (home_ref[pl.ds(c * sz.local_blocks + quarter * sz.own + i, 1), :] for c in range(3))
+        rows = (block_row(home_ref, c, None, quarter * sz.own + i) for c in range(3))
         h, m, l = features_of(*rows, (1.0, 3, 4))
         feats = jnp.concatenate([h, h, m, m, h, l, jnp.zeros((BS - DEPTH, BS), F32)], axis=0)
         out_ref[i * BS : (i + 1) * BS, :] = feats.T.astype(BF16)
@@ -129,7 +133,7 @@
     sub = lax.broadcasted_iota(jnp.int32, (BS, BS), 0)
     lane = lax.broadcasted_iota(jnp.int32, (1, BS), 1)
 
-    chunks = lax.shift_right_logical(count + BS - 1, 7)
+    chunks = jnp.maximum(lax.shift_right_logical(count + BS - 1, 7), 1)
 
     def key_of(found, slot):
         entry = jnp.where(slot < count, found.astype(jnp.int32), sz.own)
@@ -182,8 +186,12 @@
     return jnp.bitwise_and(entry, 255), lax.shift_right_logical(entry, 8)
 
 
-def tile_of(features, other_features):
-    squared = jnp.maximum(jnp.dot(features, other_features, preferred_element_type=F32), 1e-20)
+def squared_of(features, other_features):
+    return jnp.dot(features, other_features, preferred_element_type=F32)
+
+
+def taper_of(squared):
+    squared = jnp.maximum(squared, 1e-20)
     remain = jnp.maximum(4.0 - squared * lax.rsqrt(squared), 0.0)
     twice = remain * remain
     return twice * twice * (5.0 - remain)
@@ -195,17 +203,27 @@
     return first, jnp.maximum(first, last)
 
 
-def generate(sz, list_ref, count, lhs_ref, rhs_ref, tile_refs):
+def generate(sz, list_ref, count, lhs_ref, rhs_ref, tile_refs, squares):
+    top = jnp.maximum(lax.div(count + (UNROLL - 1), UNROLL) - 1, 0)
+
+    def squared(g, u):
+        i, j = entry_of(list_ref, jnp.minimum(g, top) * UNROLL + u)
+        return squared_of(
+            lhs_ref[pl.ds(pl.multiple_of(i * BS, BS), BS), :DEPTH],
+            rhs_ref[pl.ds(pl.multiple_of(j * DEPTH, DEPTH), DEPTH), :],
+        )
+
+    for u in range(UNROLL):
+        squares[u * BS : (u + 1) * BS, :] = squared(0, u)
     for at, tile_ref in enumerate(tile_refs):
 
         def group(g, unused, at=at, tile_ref=tile_ref):
             for u in range(UNROLL):
-                i, j = entry_of(list_ref, g * UNROLL + u)
+                here = slice(u * BS, (u + 1) * BS)
+                tile = taper_of(squares[here, :])
+                squares[here, :] = squared(g + 1, u)
                 start = pl.multiple_of((g * UNROLL + u - at * sz.kept) * BS, BS)
-                tile_ref[pl.ds(start, BS), :] = tile_of(
-                    lhs_ref[pl.ds(pl.multiple_of(i * BS, BS), BS), :DEPTH],
-                    rhs_ref[pl.ds(pl.multiple_of(j * DEPTH, DEPTH), DEPTH), :],
-                )
+                tile_ref[pl.ds(start, BS), :] = tile
             return unused
 
         lax.fori_loop(*kept_groups(sz, count, at), group, 0)
@@ -236,7 +254,7 @@
 
     def extra(k, unused):
         i, j = entry_of(list_ref, k)
-        tile = tile_of(*remake(i, j))
+        tile = taper_of(squared_of(*remake(i, j)))
         rows = pl.ds(pl.multiple_of(i * BS, BS), BS)
         acc[rows, :] += tile * vec_ref[pl.ds(j, 1), :]
         if acc_ones is not None:
@@ -263,11 +281,9 @@
     return jnp.sum(jnp.sum(x, axis=0, keepdims=True), axis=1, keepdims=True)
 
 
-def place_block(piece_ref, part, first, obs_ref, rhs_ref):
-    obs_ref[pl.ds(first, part), :] = piece_ref[3 * part : 4 * part, :]
-
+def place_block(piece_ref, part, first, rhs_ref):
     def one(k, unused):
-        h, m, l = features_of(*(piece_ref[pl.ds(c * part + k, 1), :] for c in range(3)), (-2.0, 4, 3))
+        h, m, l = features_of(*(block_row(piece_ref, c, part, k) for c in range(3)), (-2.0, 4, 3))
         feats = jnp.concatenate([h, m, h, m, l, h], axis=0).astype(BF16)
         rhs_ref[pl.ds(pl.multiple_of((first + k) * DEPTH, DEPTH), DEPTH), :] = feats
         return unused
@@ -276,25 +292,34 @@
 
 
 def first_kernel(sz, *refs):
-    list_ref, count_ref, lhs_ref, nugget_ref, home_ref = refs[:5]
-    coord_refs = refs[4 : 5 + (sz.blks - 1) * sz.reps]
-    refs = refs[5 + (sz.blks - 1) * sz.reps :]
+    list_ref, count_ref, lhs_ref, nugget_any, obs_any, home_ref = refs[:6]
+    coord_refs = refs[6 : 6 + (sz.blks - 1) * sz.reps]
+    refs = refs[6 + (sz.blks - 1) * sz.reps :]
     tile_refs = refs[:ARRAYS]
-    spare_ref, obs_ref, diag_ref, mapped_ref, norm_ref, rhs_ref, acc, acc_ones, total_row, done = refs[ARRAYS:]
+    spare_ref, obs_ref, diag_ref, mapped_ref, norm_ref = refs[ARRAYS : ARRAYS + 5]
+    rhs_ref, acc, acc_ones, total_row, squares, nugget_ref, done, fetched = refs[ARRAYS + 5 :]
     blk, rep = lax.axis_index("blk"), lax.axis_index("rep")
-    for at, piece_ref in enumerate(coord_refs[1:]):
+    home = pl.ds(pl.multiple_of(blk * sz.local_blocks, 8), sz.local_blocks)
+    fetch = pltpu.make_async_copy(nugget_any, nugget_ref, fetched.at[0])
+    fetch_obs = pltpu.make_async_copy(obs_any, obs_ref.at[home, :], fetched.at[1])
+    fetch.start()
+    fetch_obs.start()
+    for at, piece_ref in enumerate(coord_refs):
         code, turn = at // sz.reps + 1, at % sz.reps
         part = sz.local_blocks // sz.reps
         first = jnp.bitwise_xor(blk, code) * sz.local_blocks + jnp.bitwise_xor(rep, turn) * part
-        place_block(piece_ref, part, pl.multiple_of(first, 8), obs_ref, rhs_ref)
-    place_block(home_ref, sz.local_blocks, pl.multiple_of(blk * sz.local_blocks, 8), obs_ref, rhs_ref)
+        first = pl.multiple_of(first, 8)
+        place_block(piece_ref, part, first, rhs_ref)
+        obs_ref[pl.ds(first, part), :] = piece_ref[3 * part : 4 * part, :]
+    place_block(home_ref, sz.local_blocks, blk * sz.local_blocks, rhs_ref)
     count = count_ref[0]
-    generate(sz, list_ref, count, lhs_ref, rhs_ref, tile_refs)
+    generate(sz, list_ref, count, lhs_ref, rhs_ref, tile_refs, squares)
 
     def remake(i, j):
         features = lhs_ref[pl.ds(pl.multiple_of(i * BS, BS), BS), :DEPTH]
         return features, rhs_ref[pl.ds(pl.multiple_of(j * DEPTH, DEPTH), DEPTH), :]
 
+    fetch_obs.wait()
     sweep(sz, list_ref, count, tile_refs, obs_ref, acc, acc_ones, remake)
 
     @pl.when(count > sz.kept * ARRAYS)
@@ -307,6 +332,7 @@
     finish(sz, acc, mapped_ref)
     quarter = lax.axis_index("col") * sz.reps + rep
     own = pl.ds(pl.multiple_of(sz.me() * sz.own, 8), sz.own)
+    fetch.wait()
     diag = nugget_ref[pl.ds(pl.multiple_of(quarter * sz.own, 8), sz.own), :] + total_row[...]
     diag_ref[...] = diag
     mapped_ref[...] += diag * obs_ref[own, :]
@@ -397,9 +423,10 @@
     pairs = jnp.where(alive, tile_pairs, -1).reshape(2 * sz.slots // BS, BS)
     rep = lax.axis_index("rep")
     part = home // sz.reps
-    rows = jnp.concatenate([coords, observations[None]], axis=0).reshape(4, home, BS)
-    half = lax.dynamic_slice_in_dim(rows, rep * part, part, axis=1).reshape(4 * part, BS)
-    rows = rows.reshape(4 * home, BS)
+    obs_rows = observations.reshape(home, BS)
+    rows = coords.reshape(3, home, BS)
+    half = lax.dynamic_slice_in_dim(jnp.concatenate([rows, obs_rows[None]], axis=0), rep * part, part, axis=1)
+    half = half.reshape(4 * part, BS)
     nears = [swap(half, "blk", z) for z in range(1, sz.blks)]
     pair_arrays = over_plane(along_blk(pairs))
 
@@ -436,7 +463,7 @@
     *tiles, spare, obs, diag, mapped, norm = call(
         functools.partial(first_kernel, sz),
         sz.first_mib,
-        [SMEM, SMEM] + [VMEM] * (3 + len(coord_arrays)),
+        [SMEM, SMEM, VMEM, ANY, ANY] + [VMEM] * (1 + len(coord_arrays)),
         kept
         + [
             pltpu.HBM((blocks * DEPTH, BS), BF16),
@@ -451,13 +478,17 @@
             tall,
             tall,
             pltpu.VMEM((own, BS), F32),
+            pltpu.VMEM((UNROLL * BS, BS), F32),
+            pltpu.VMEM((home, BS), F32),
             pltpu.SemaphoreType.DMA,
+            pltpu.SemaphoreType.DMA((2,)),
         ],
         100_000_000,
         table,
         count,
         lhs,
-        nugget.reshape(home, BS),
+        pltpu.with_memory_space_constraint(nugget.reshape(home, BS), pltpu.HBM),
+        pltpu.with_memory_space_constraint(obs_rows, pltpu.HBM),
         rows,
         *coord_arrays,
     )

time: 118 us -> 110 us (0.932)
  the two profiles are of different devices: /device:TPU:13 before, /device:TPU:0 now
where the time goes in v2:
time: 110 us; the launch traced here: 109 us
  Pallas kernels  48.6 us (44%)
  starting transfers between devices  30.6 us (28%)
  waiting for transfers between devices  25.5 us (23%)
  other arithmetic  1.48 us (1%)
  between operations  1.43 us (1%)
    pallas_call x6, Pallas kernels, call(): pl.pallas_call(kernel, in_specs=in_specs, out_shape=shapes, out_specs=out...  48.6 us
    ppermute x30, starting transfers between devices, swap(): lax.ppermute(x, axis, [(i, i ^ code) for i in range(lax.axis_size(axis))])  30.6 us
    ppermute x30, waiting for transfers between devices, swap(): lax.ppermute(x, axis, [(i, i ^ code) for i in range(lax.axis_size(axis))])  25.5 us
  transfers between devices with their start and end apart: 30, of which 15 were waited for; matrix products, arithmetic and copies ran while one was open for 2% of the time, Pallas kernels for 3%

profile of v2, /device:TPU:0, one launch (start us, length us, event | category | flops | bytes accessed | tf_op | source)
XLA Modules:
  0.0 108.6 jit_solution(1865862020924260431)
XLA Ops:
  1.3 0.7 broadcast_select_fusion
  2.0 5.0 %collective-permute-start.2 = (s32[4,128]{1,0:T(4,128)S(1)}, s32[4,128]{1,0:T(4,128)S(1)}, u32[]{:S(2)}, u32[]{:S(2)}) collective-permute-start(s32[4,128]{1,0:T(4,128)S(1)} %reshape.28), channel_id=1, source_target_pairs={{0,12},{4,8},{8,4},{12,0},{1,13},{5,9},{9,5},{13,1},{2,14},{6,10},... | collective-permute-start | bytes 6152 | tf_op jit(solution)/shard_map/ppermute | solution.py:48
  7.0 0.0 collective-permute-start.1
  7.0 0.6 collective-permute-start
  7.7 1.0 copy.9
  8.6 0.8 fusion
  9.4 3.8 %collective-permute-start.8 = (f32[256,128]{1,0:T(8,128)S(1)}, f32[256,128]{1,0:T(8,128)S(1)}, u32[]{:S(2)}, u32[]{:S(2)}) collective-permute-start(f32[256,128]{1,0:T(8,128)S(1)} %bitcast.22), channel_id=1, source_target_pairs={{0,12},{4,8},{8,4},{12,0},{1,13},{5,9},{9,5},{13,1},{2,14},{6,10},... | collective-permute-start | bytes 393224 | tf_op jit(solution)/shard_map/ppermute | solution.py:48
  13.2 0.6 collective-permute-start.6
  13.9 1.7 %collective-permute-start.4 = (s32[16,128]{1,0:T(8,128)S(1)}, s32[16,128]{1,0:T(8,128)S(1)}, u32[]{:S(2)}, u32[]{:S(2)}) collective-permute-start(s32[16,128]{1,0:T(8,128)S(1)} %pad_add_fusion.refs_0_), channel_id=1, source_target_pairs={{0,2},{2,0},{1,3},{3,1},{4,6},{6,4},{5,7},{7,5},{8,10},{10,8},{9,1... | collective-permute-start | bytes 24584 | tf_op jit(solution)/shard_map/ppermute | solution.py:48
  15.6 2.0 %collective-permute-done.4.refs_2_ = s32[16,128]{1,0:T(8,128)S(1)} collective-permute-done((s32[16,128]{1,0:T(8,128)S(1)}, s32[16,128]{1,0:T(8,128)S(1)}, u32[]{:S(2)}, u32[]{:S(2)}) %collective-permute-start.4) | collective-permute-done | bytes 8224 | tf_op jit(solution)/shard_map/ppermute | solution.py:48
  17.6 0.0 collective-permute-start.5
  17.6 0.4 shard_map.69.refs_2_
  18.0 0.0 collective-permute-done.3.refs_1_
  18.0 0.8 collective-permute-done.5.refs_3_
  18.8 3.0 %shard_map.68 = (s32[16,128]{1,0:T(8,128)S(1)}, s32[1]{0:T(128)}) custom-call(s32[16,128]{1,0:T(8,128)S(1)} %pad_add_fusion.refs_0_, s32[16,128]{1,0:T(8,128)S(1)} %collective-permute-done.3.refs_1_, s32[16,128]{1,0:T(8,128)S(1)} %collective-permute-done.4.refs_2_, s32[16,128]{1,0:T(8,128)S(1)} %collective-permute-done.5.refs_3_), custom_call_target="tpu_custom_call" | custom-call | flops 10000000 | bytes 1048576 | tf_op jit(solution)/shard_map/pallas_call | solution.py:404
  21.8 0.0 collective-permute-done.8.refs_10_
  21.8 1.6 %collective-permute-done.7.refs_8_ = f32[256,128]{1,0:T(8,128)S(1)} collective-permute-done((f32[256,128]{1,0:T(8,128)S(1)}, f32[256,128]{1,0:T(8,128)S(1)}, u32[]{:S(2)}, u32[]{:S(2)}) %collective-permute-start.7) | collective-permute-done | bytes 131104 | tf_op jit(solution)/shard_map/ppermute | solution.py:48
  23.4 0.5 collective-permute-start.10
  23.9 0.0 collective-permute-start.11
  23.9 0.8 collective-permute-done.9.refs_7_
  24.8 0.2 collective-permute-done.10.refs_9_
  25.0 0.3 collective-permute-done.11.refs_11_
  25.3 30.4 %shard_map.70 = (f32[14336,128]{1,0:T(8,128)S(1)}, f32[14336,128]{1,0:T(8,128)S(1)}, f32[14336,128]{1,0:T(8,128)S(1)}, f32[14336,128]{1,0:T(8,128)S(1)}, bf16[24...) custom-call(s32[2048]{0:T(1024)S(1)} %bitcast.16, ...), custom_call_target="tpu_custom_call" | custom-call | flops 100000000 | bytes 1048576 | tf_op jit(solution)/shard_map/pallas_call | solution.py:404
  55.7 0.1 collective-permute-start.14
  55.8 4.1 %collective-permute-start.13 = (f32[32,128]{1,0:T(8,128)S(1)}, f32[32,128]{1,0:T(8,128)S(1)}, u32[]{:S(2)}, u32[]{:S(2)}) collective-permute-start(f32[32,128]{1,0:T(8,128)S(1)} %get-tuple-element.42), channel_id=1, source_target_pairs={{0,8},{4,12},{8,0},{12,4},{1,9},{5,13},{9,1},{13,5},{2,10},{6,14},... | collective-permute-start | bytes 49160 | tf_op jit(solution)/shard_map/ppermute | solution.py:48
  59.9 0.5 collective-permute-start.12
  60.4 3.2 %collective-permute-done.12 = f32[32,128]{1,0:T(8,128)S(1)} collective-permute-done((f32[32,128]{1,0:T(8,128)S(1)}, f32[32,128]{1,0:T(8,128)S(1)}, u32[]{:S(2)}, u32[]{:S(2)}) %collective-permute-start.12) | collective-permute-done | bytes 16416 | tf_op jit(solution)/shard_map/ppermute | solution.py:48
  63.7 1.8 %collective-permute-start.16 = (f32[128,128]{1,0:T(8,128)S(1)}, f32[128,128]{1,0:T(8,128)S(1)}, u32[]{:S(2)}, u32[]{:S(2)}) collective-permute-start(f32[128,128]{1,0:T(8,128)S(1)} %constant_dynamic-update-slice_fusion.refs_9_), channel_id=1, source_target_pairs={{0,2},{2,0},{1,3},{3,1},{4,6},{6,4},{5,7},{7,5},{8,10},{10,8},{9,1... | collective-permute-start | bytes 196616 | tf_op jit(solution)/shard_map/ppermute | solution.py:48
  65.5 0.0 collective-permute-start.15
  65.5 2.5 %collective-permute-done.16.refs_11_ = f32[128,128]{1,0:T(8,128)S(1)} collective-permute-done((f32[128,128]{1,0:T(8,128)S(1)}, f32[128,128]{1,0:T(8,128)S(1)}, u32[]{:S(2)}, u32[]{:S(2)}) %collective-permute-start.16) | collective-permute-done | bytes 65568 | tf_op jit(solution)/shard_map/ppermute | solution.py:48
  68.0 1.2 %collective-permute-done.17.refs_12_ = f32[128,128]{1,0:T(8,128)S(1)} collective-permute-done((f32[128,128]{1,0:T(8,128)S(1)}, f32[128,128]{1,0:T(8,128)S(1)}, u32[]{:S(2)}, u32[]{:S(2)}) %collective-permute-start.17) | collective-permute-done | bytes 65568 | tf_op jit(solution)/shard_map/ppermute | solution.py:48
  69.3 7.0 %shard_map.71 = (f32[32,128]{1,0:T(8,128)S(1)}, f32[8,128]{1,0:T(8,128)S(1)}, f32[128,128]{1,0:T(8,128)S(1)}, f32[512,128]{1,0:T(8,128)S(1)}, f32[512,128]{1,0:T(8,128)S(1)}) custom-call(s32[2048]{0:T(1024)S(1)} %bitcast.17, s32[1]{0:T(128)} %get-tuple-element.33.refs_1_, bf16[4224,128]{1,0:T(8,128)(2,1)S(1)} %shard_map.69.refs_2_, ...), custom_call_target="tpu_custom_call" | custom-call | flops 100000000 | bytes 1048576 | tf_op jit(solution)/shard_map/pallas_call | solution.py:404
  76.3 2.1 %collective-permute-start.20 = (f32[32,128]{1,0:T(8,128)S(1)}, f32[32,128]{1,0:T(8,128)S(1)}, u32[]{:S(2)}, u32[]{:S(2)}) collective-permute-start(f32[32,128]{1,0:T(8,128)S(1)} %get-tuple-element.51), channel_id=1, source_target_pairs={{0,12},{4,8},{8,4},{12,0},{1,13},{5,9},{9,5},{13,1},{2,14},{6,10},... | collective-permute-start | bytes 49160 | tf_op jit(solution)/shard_map/ppermute | solution.py:48
  78.3 1.2 %collective-permute-start.19 = (f32[32,128]{1,0:T(8,128)S(1)}, f32[32,128]{1,0:T(8,128)S(1)}, u32[]{:S(2)}, u32[]{:S(2)}) collective-permute-start(f32[32,128]{1,0:T(8,128)S(1)} %get-tuple-element.51), channel_id=1, source_target_pairs={{0,8},{4,12},{8,0},{12,4},{1,9},{5,13},{9,1},{13,5},{2,10},{6,14},... | collective-permute-start | bytes 49160 | tf_op jit(solution)/shard_map/ppermute | solution.py:48
  79.5 1.2 %collective-permute-start.18 = (f32[32,128]{1,0:T(8,128)S(1)}, f32[32,128]{1,0:T(8,128)S(1)}, u32[]{:S(2)}, u32[]{:S(2)}) collective-permute-start(f32[32,128]{1,0:T(8,128)S(1)} %get-tuple-element.51), channel_id=1, source_target_pairs={{0,4},{4,0},{8,12},{12,8},{1,5},{5,1},{9,13},{13,9},{2,6},{6,2},{1... | collective-permute-start | bytes 49160 | tf_op jit(solution)/shard_map/ppermute | solution.py:48
  80.7 2.6 %collective-permute-done.18 = f32[32,128]{1,0:T(8,128)S(1)} collective-permute-done((f32[32,128]{1,0:T(8,128)S(1)}, f32[32,128]{1,0:T(8,128)S(1)}, u32[]{:S(2)}, u32[]{:S(2)}) %collective-permute-start.18) | collective-permute-done | bytes 16416 | tf_op jit(solution)/shard_map/ppermute | solution.py:48
  83.4 1.0 collective-permute-start.22
  84.3 3.3 %collective-permute-done.22.refs_11_ = f32[128,128]{1,0:T(8,128)S(1)} collective-permute-done((f32[128,128]{1,0:T(8,128)S(1)}, f32[128,128]{1,0:T(8,128)S(1)}, u32[]{:S(2)}, u32[]{:S(2)}) %collective-permute-start.22) | collective-permute-done | bytes 65568 | tf_op jit(solution)/shard_map/ppermute | solution.py:48
  87.7 1.2 %collective-permute-done.23.refs_12_ = f32[128,128]{1,0:T(8,128)S(1)} collective-permute-done((f32[128,128]{1,0:T(8,128)S(1)}, f32[128,128]{1,0:T(8,128)S(1)}, u32[]{:S(2)}, u32[]{:S(2)}) %collective-permute-start.23) | collective-permute-done | bytes 65568 | tf_op jit(solution)/shard_map/ppermute | solution.py:48
  88.9 7.1 %shard_map.72 = (f32[32,128]{1,0:T(8,128)S(1)}, f32[8,128]{1,0:T(8,128)S(1)}, f32[128,128]{1,0:T(8,128)S(1)}, f32[128,128]{1,0:T(8,128)S(1)}, f32[128,128]{1,0:T(8,128)S(1)}, /*index=5*/f32[8,128]{1,0:T(8,128)S(1)}) custom-call(s32[2048]{0:T(1024)S(1)} %bitcast.18, s32[1]{0:T(128)} %get-tuple-element.33.refs_1_, bf16[4224,128]{1,0:T(8,128)(2,1)S(1)} %shard_map.69.refs_2_, ...), custom_call_target="tpu_custom_call" | custom-call | flops 100000000 | bytes 1048576 | tf_op jit(solution)/shard_map/pallas_call | solution.py:404
  96.1 0.9 collective-permute-start.26
  97.0 2.1 %collective-permute-start.25 = (f32[8,128]{1,0:T(8,128)S(1)}, f32[8,128]{1,0:T(8,128)S(1)}, u32[]{:S(2)}, u32[]{:S(2)}) collective-permute-start(f32[8,128]{1,0:T(8,128)S(1)} %get-tuple-element.57), channel_id=1, source_target_pairs={{0,8},{4,12},{8,0},{12,4},{1,9},{5,13},{9,1},{13,5},{2,10},{6,14},... | collective-permute-start | bytes 12296 | tf_op jit(solution)/shard_map/ppermute | solution.py:48
  99.1 1.4 %collective-permute-start.24 = (f32[8,128]{1,0:T(8,128)S(1)}, f32[8,128]{1,0:T(8,128)S(1)}, u32[]{:S(2)}, u32[]{:S(2)}) collective-permute-start(f32[8,128]{1,0:T(8,128)S(1)} %get-tuple-element.57), channel_id=1, source_target_pairs={{0,4},{4,0},{8,12},{12,8},{1,5},{5,1},{9,13},{13,9},{2,6},{6,2},{1... | collective-permute-start | bytes 12296 | tf_op jit(solution)/shard_map/ppermute | solution.py:48
  100.5 2.2 %collective-permute-done.24 = f32[8,128]{1,0:T(8,128)S(1)} collective-permute-done((f32[8,128]{1,0:T(8,128)S(1)}, f32[8,128]{1,0:T(8,128)S(1)}, u32[]{:S(2)}, u32[]{:S(2)}) %collective-permute-start.24) | collective-permute-done | bytes 4128 | tf_op jit(solution)/shard_map/ppermute | solution.py:48
  102.7 1.9 %collective-permute-start.28 = (f32[64,128]{1,0:T(8,128)S(1)}, f32[64,128]{1,0:T(8,128)S(1)}, u32[]{:S(2)}, u32[]{:S(2)}) collective-permute-start(f32[64,128]{1,0:T(8,128)S(1)} %constant_dynamic-update-slice_fusion.8.refs_4_), channel_id=1, source_target_pairs={{0,2},{2,0},{1,3},{3,1},{4,6},{6,4},{5,7},{7,5},{8,10},{10,8},{9,1... | collective-permute-start | bytes 98312 | tf_op jit(solution)/shard_map/ppermute | solution.py:48
  104.6 2.1 %collective-permute-done.28.refs_6_ = f32[64,128]{1,0:T(8,128)S(1)} collective-permute-done((f32[64,128]{1,0:T(8,128)S(1)}, f32[64,128]{1,0:T(8,128)S(1)}, u32[]{:S(2)}, u32[]{:S(2)}) %collective-permute-start.28) | collective-permute-done | bytes 32800 | tf_op jit(solution)/shard_map/ppermute | solution.py:48
  106.7 1.2 %collective-permute-done.29.refs_7_ = f32[64,128]{1,0:T(8,128)S(1)} collective-permute-done((f32[64,128]{1,0:T(8,128)S(1)}, f32[64,128]{1,0:T(8,128)S(1)}, u32[]{:S(2)}, u32[]{:S(2)}) %collective-permute-start.29) | collective-permute-done | bytes 32800 | tf_op jit(solution)/shard_map/ppermute | solution.py:48
  107.9 0.7 shard_map.73
  (37 shorter events, 0.1 us)
Async XLA Ops:
  2.0 11.3 %collective-permute-start.2 = (s32[4,128]{1,0:T(4,128)S(1)}, s32[4,128]{1,0:T(4,128)S(1)}, u32[]{:S(2)}, u32[]{:S(2)}) collective-permute-start(s32[4,128]{1,0:T(4,128)S(1)} %reshape.28), channel_id=1, source_target_pairs={{0,12},{4,8},{8,4},{12,0},{1,13},{5,9},{9,5},{13,1},{2,14},{6,10},... | collective-permute-start | bytes 6152 | tf_op jit(solution)/shard_map/ppermute | solution.py:48
  7.0 6.8 %collective-permute-start.1 = (s32[4,128]{1,0:T(4,128)S(1)}, s32[4,128]{1,0:T(4,128)S(1)}, u32[]{:S(2)}, u32[]{:S(2)}) collective-permute-start(s32[4,128]{1,0:T(4,128)S(1)} %reshape.28), channel_id=1, source_target_pairs={{0,8},{4,12},{8,0},{12,4},{1,9},{5,13},{9,1},{13,5},{2,10},{6,14},... | collective-permute-start | bytes 6152 | tf_op jit(solution)/shard_map/ppermute | solution.py:48
  7.0 6.8 %collective-permute-start = (s32[4,128]{1,0:T(4,128)S(1)}, s32[4,128]{1,0:T(4,128)S(1)}, u32[]{:S(2)}, u32[]{:S(2)}) collective-permute-start(s32[4,128]{1,0:T(4,128)S(1)} %reshape.28), channel_id=1, source_target_pairs={{0,4},{4,0},{8,12},{12,8},{1,5},{5,1},{9,13},{13,9},{2,6},{6,2},{1... | collective-permute-start | bytes 6152 | tf_op jit(solution)/shard_map/ppermute | solution.py:48
  9.4 12.4 %collective-permute-start.8 = (f32[256,128]{1,0:T(8,128)S(1)}, f32[256,128]{1,0:T(8,128)S(1)}, u32[]{:S(2)}, u32[]{:S(2)}) collective-permute-start(f32[256,128]{1,0:T(8,128)S(1)} %bitcast.22), channel_id=1, source_target_pairs={{0,12},{4,8},{8,4},{12,0},{1,13},{5,9},{9,5},{13,1},{2,14},{6,10},... | collective-permute-start | bytes 393224 | tf_op jit(solution)/shard_map/ppermute | solution.py:48
  13.2 10.2 %collective-permute-start.7 = (f32[256,128]{1,0:T(8,128)S(1)}, f32[256,128]{1,0:T(8,128)S(1)}, u32[]{:S(2)}, u32[]{:S(2)}) collective-permute-start(f32[256,128]{1,0:T(8,128)S(1)} %bitcast.23), channel_id=1, source_target_pairs={{0,8},{4,12},{8,0},{12,4},{1,9},{5,13},{9,1},{13,5},{2,10},{6,14},... | collective-permute-start | bytes 393224 | tf_op jit(solution)/shard_map/ppermute | solution.py:48
  13.2 10.2 %collective-permute-start.6 = (f32[256,128]{1,0:T(8,128)S(1)}, f32[256,128]{1,0:T(8,128)S(1)}, u32[]{:S(2)}, u32[]{:S(2)}) collective-permute-start(f32[256,128]{1,0:T(8,128)S(1)} %bitcast.24), channel_id=1, source_target_pairs={{0,4},{4,0},{8,12},{12,8},{1,5},{5,1},{9,13},{13,9},{2,6},{6,2},{1... | collective-permute-start | bytes 393224 | tf_op jit(solution)/shard_map/ppermute | solution.py:48
  13.9 3.7 %collective-permute-start.4 = (s32[16,128]{1,0:T(8,128)S(1)}, s32[16,128]{1,0:T(8,128)S(1)}, u32[]{:S(2)}, u32[]{:S(2)}) collective-permute-start(s32[16,128]{1,0:T(8,128)S(1)} %pad_add_fusion.refs_0_), channel_id=1, source_target_pairs={{0,2},{2,0},{1,3},{3,1},{4,6},{6,4},{5,7},{7,5},{8,10},{10,8},{9,1... | collective-permute-start | bytes 24584 | tf_op jit(solution)/shard_map/ppermute | solution.py:48
  15.6 2.4 %collective-permute-start.3 = (s32[16,128]{1,0:T(8,128)S(1)}, s32[16,128]{1,0:T(8,128)S(1)}, u32[]{:S(2)}, u32[]{:S(2)}) collective-permute-start(s32[16,128]{1,0:T(8,128)S(1)} %pad_add_fusion.refs_0_), channel_id=1, source_target_pairs={{0,1},{1,0},{2,3},{3,2},{4,5},{5,4},{6,7},{7,6},{8,9},{9,8},{10,11... | collective-permute-start | bytes 24584 | tf_op jit(solution)/shard_map/ppermute | solution.py:48
  17.6 1.2 %collective-permute-start.5 = (s32[16,128]{1,0:T(8,128)S(1)}, s32[16,128]{1,0:T(8,128)S(1)}, u32[]{:S(2)}, u32[]{:S(2)}) collective-permute-start(s32[16,128]{1,0:T(8,128)S(1)} %collective-permute-done.4.refs_2_), channel_id=1, source_target_pairs={{0,1},{1,0},{2,3},{3,2},{4,5},{5,4},{6,7},{7,6},{8,9},{9,8},{10,11... | collective-permute-start | bytes 24584 | tf_op jit(solution)/shard_map/ppermute | solution.py:48
  23.4 1.3 %collective-permute-start.9 = (f32[256,128]{1,0:T(8,128)S(1)}, f32[256,128]{1,0:T(8,128)S(1)}, u32[]{:S(2)}, u32[]{:S(2)}) collective-permute-start(f32[256,128]{1,0:T(8,128)S(1)} %collective-permute-done.6.refs_6_), channel_id=1, source_target_pairs={{0,1},{1,0},{2,3},{3,2},{4,5},{5,4},{6,7},{7,6},{8,9},{9,8},{10,11... | collective-permute-start | bytes 393224 | tf_op jit(solution)/shard_map/ppermute | solution.py:48
  23.4 1.5 %collective-permute-start.10 = (f32[256,128]{1,0:T(8,128)S(1)}, f32[256,128]{1,0:T(8,128)S(1)}, u32[]{:S(2)}, u32[]{:S(2)}) collective-permute-start(f32[256,128]{1,0:T(8,128)S(1)} %collective-permute-done.7.refs_8_), channel_id=1, source_target_pairs={{0,1},{1,0},{2,3},{3,2},{4,5},{5,4},{6,7},{7,6},{8,9},{9,8},{10,11... | collective-permute-start | bytes 393224 | tf_op jit(solution)/shard_map/ppermute | solution.py:48
  23.9 1.3 %collective-permute-start.11 = (f32[256,128]{1,0:T(8,128)S(1)}, f32[256,128]{1,0:T(8,128)S(1)}, u32[]{:S(2)}, u32[]{:S(2)}) collective-permute-start(f32[256,128]{1,0:T(8,128)S(1)} %collective-permute-done.8.refs_10_), channel_id=1, source_target_pairs={{0,1},{1,0},{2,3},{3,2},{4,5},{5,4},{6,7},{7,6},{8,9},{9,8},{10,11... | collective-permute-start | bytes 393224 | tf_op jit(solution)/shard_map/ppermute | solution.py:48
  55.7 7.9 %collective-permute-start.14 = (f32[32,128]{1,0:T(8,128)S(1)}, f32[32,128]{1,0:T(8,128)S(1)}, u32[]{:S(2)}, u32[]{:S(2)}) collective-permute-start(f32[32,128]{1,0:T(8,128)S(1)} %get-tuple-element.42), channel_id=1, source_target_pairs={{0,12},{4,8},{8,4},{12,0},{1,13},{5,9},{9,5},{13,1},{2,14},{6,10},... | collective-permute-start | bytes 49160 | tf_op jit(solution)/shard_map/ppermute | solution.py:48
  55.8 7.9 %collective-permute-start.13 = (f32[32,128]{1,0:T(8,128)S(1)}, f32[32,128]{1,0:T(8,128)S(1)}, u32[]{:S(2)}, u32[]{:S(2)}) collective-permute-start(f32[32,128]{1,0:T(8,128)S(1)} %get-tuple-element.42), channel_id=1, source_target_pairs={{0,8},{4,12},{8,0},{12,4},{1,9},{5,13},{9,1},{13,5},{2,10},{6,14},... | collective-permute-start | bytes 49160 | tf_op jit(solution)/shard_map/ppermute | solution.py:48
  59.9 3.7 %collective-permute-start.12 = (f32[32,128]{1,0:T(8,128)S(1)}, f32[32,128]{1,0:T(8,128)S(1)}, u32[]{:S(2)}, u32[]{:S(2)}) collective-permute-start(f32[32,128]{1,0:T(8,128)S(1)} %get-tuple-element.42), channel_id=1, source_target_pairs={{0,4},{4,0},{8,12},{12,8},{1,5},{5,1},{9,13},{13,9},{2,6},{6,2},{1... | collective-permute-start | bytes 49160 | tf_op jit(solution)/shard_map/ppermute | solution.py:48
  63.7 4.3 %collective-permute-start.16 = (f32[128,128]{1,0:T(8,128)S(1)}, f32[128,128]{1,0:T(8,128)S(1)}, u32[]{:S(2)}, u32[]{:S(2)}) collective-permute-start(f32[128,128]{1,0:T(8,128)S(1)} %constant_dynamic-update-slice_fusion.refs_9_), channel_id=1, source_target_pairs={{0,2},{2,0},{1,3},{3,1},{4,6},{6,4},{5,7},{7,5},{8,10},{10,8},{9,1... | collective-permute-start | bytes 196616 | tf_op jit(solution)/shard_map/ppermute | solution.py:48
  65.5 2.6 %collective-permute-start.15 = (f32[128,128]{1,0:T(8,128)S(1)}, f32[128,128]{1,0:T(8,128)S(1)}, u32[]{:S(2)}, u32[]{:S(2)}) collective-permute-start(f32[128,128]{1,0:T(8,128)S(1)} %constant_dynamic-update-slice_fusion.refs_9_), channel_id=1, source_target_pairs={{0,1},{1,0},{2,3},{3,2},{4,5},{5,4},{6,7},{7,6},{8,9},{9,8},{10,11... | collective-permute-start | bytes 196616 | tf_op jit(solution)/shard_map/ppermute | solution.py:48
  68.0 1.3 %collective-permute-start.17 = (f32[128,128]{1,0:T(8,128)S(1)}, f32[128,128]{1,0:T(8,128)S(1)}, u32[]{:S(2)}, u32[]{:S(2)}) collective-permute-start(f32[128,128]{1,0:T(8,128)S(1)} %collective-permute-done.16.refs_11_), channel_id=1, source_target_pairs={{0,1},{1,0},{2,3},{3,2},{4,5},{5,4},{6,7},{7,6},{8,9},{9,8},{10,11... | collective-permute-start | bytes 196616 | tf_op jit(solution)/shard_map/ppermute | solution.py:48
  76.3 7.1 %collective-permute-start.20 = (f32[32,128]{1,0:T(8,128)S(1)}, f32[32,128]{1,0:T(8,128)S(1)}, u32[]{:S(2)}, u32[]{:S(2)}) collective-permute-start(f32[32,128]{1,0:T(8,128)S(1)} %get-tuple-element.51), channel_id=1, source_target_pairs={{0,12},{4,8},{8,4},{12,0},{1,13},{5,9},{9,5},{13,1},{2,14},{6,10},... | collective-permute-start | bytes 49160 | tf_op jit(solution)/shard_map/ppermute | solution.py:48
  78.3 5.0 %collective-permute-start.19 = (f32[32,128]{1,0:T(8,128)S(1)}, f32[32,128]{1,0:T(8,128)S(1)}, u32[]{:S(2)}, u32[]{:S(2)}) collective-permute-start(f32[32,128]{1,0:T(8,128)S(1)} %get-tuple-element.51), channel_id=1, source_target_pairs={{0,8},{4,12},{8,0},{12,4},{1,9},{5,13},{9,1},{13,5},{2,10},{6,14},... | collective-permute-start | bytes 49160 | tf_op jit(solution)/shard_map/ppermute | solution.py:48
  79.5 3.8 %collective-permute-start.18 = (f32[32,128]{1,0:T(8,128)S(1)}, f32[32,128]{1,0:T(8,128)S(1)}, u32[]{:S(2)}, u32[]{:S(2)}) collective-permute-start(f32[32,128]{1,0:T(8,128)S(1)} %get-tuple-element.51), channel_id=1, source_target_pairs={{0,4},{4,0},{8,12},{12,8},{1,5},{5,1},{9,13},{13,9},{2,6},{6,2},{1... | collective-permute-start | bytes 49160 | tf_op jit(solution)/shard_map/ppermute | solution.py:48
  83.4 4.3 %collective-permute-start.22 = (f32[128,128]{1,0:T(8,128)S(1)}, f32[128,128]{1,0:T(8,128)S(1)}, u32[]{:S(2)}, u32[]{:S(2)}) collective-permute-start(f32[128,128]{1,0:T(8,128)S(1)} %constant_dynamic-update-slice_fusion.4.refs_9_), channel_id=1, source_target_pairs={{0,2},{2,0},{1,3},{3,1},{4,6},{6,4},{5,7},{7,5},{8,10},{10,8},{9,1... | collective-permute-start | bytes 196616 | tf_op jit(solution)/shard_map/ppermute | solution.py:48
  84.3 3.4 %collective-permute-start.21 = (f32[128,128]{1,0:T(8,128)S(1)}, f32[128,128]{1,0:T(8,128)S(1)}, u32[]{:S(2)}, u32[]{:S(2)}) collective-permute-start(f32[128,128]{1,0:T(8,128)S(1)} %constant_dynamic-update-slice_fusion.4.refs_9_), channel_id=1, source_target_pairs={{0,1},{1,0},{2,3},{3,2},{4,5},{5,4},{6,7},{7,6},{8,9},{9,8},{10,11... | collective-permute-start | bytes 196616 | tf_op jit(solution)/shard_map/ppermute | solution.py:48
  87.7 1.3 %collective-permute-start.23 = (f32[128,128]{1,0:T(8,128)S(1)}, f32[128,128]{1,0:T(8,128)S(1)}, u32[]{:S(2)}, u32[]{:S(2)}) collective-permute-start(f32[128,128]{1,0:T(8,128)S(1)} %collective-permute-done.22.refs_11_), channel_id=1, source_target_pairs={{0,1},{1,0},{2,3},{3,2},{4,5},{5,4},{6,7},{7,6},{8,9},{9,8},{10,11... | collective-permute-start | bytes 196616 | tf_op jit(solution)/shard_map/ppermute | solution.py:48
  96.1 6.6 %collective-permute-start.26 = (f32[8,128]{1,0:T(8,128)S(1)}, f32[8,128]{1,0:T(8,128)S(1)}, u32[]{:S(2)}, u32[]{:S(2)}) collective-permute-start(f32[8,128]{1,0:T(8,128)S(1)} %get-tuple-element.57), channel_id=1, source_target_pairs={{0,12},{4,8},{8,4},{12,0},{1,13},{5,9},{9,5},{13,1},{2,14},{6,10},... | collective-permute-start | bytes 12296 | tf_op jit(solution)/shard_map/ppermute | solution.py:48
  97.0 5.7 %collective-permute-start.25 = (f32[8,128]{1,0:T(8,128)S(1)}, f32[8,128]{1,0:T(8,128)S(1)}, u32[]{:S(2)}, u32[]{:S(2)}) collective-permute-start(f32[8,128]{1,0:T(8,128)S(1)} %get-tuple-element.57), channel_id=1, source_target_pairs={{0,8},{4,12},{8,0},{12,4},{1,9},{5,13},{9,1},{13,5},{2,10},{6,14},... | collective-permute-start | bytes 12296 | tf_op jit(solution)/shard_map/ppermute | solution.py:48
  99.1 3.6 %collective-permute-start.24 = (f32[8,128]{1,0:T(8,128)S(1)}, f32[8,128]{1,0:T(8,128)S(1)}, u32[]{:S(2)}, u32[]{:S(2)}) collective-permute-start(f32[8,128]{1,0:T(8,128)S(1)} %get-tuple-element.57), channel_id=1, source_target_pairs={{0,4},{4,0},{8,12},{12,8},{1,5},{5,1},{9,13},{13,9},{2,6},{6,2},{1... | collective-permute-start | bytes 12296 | tf_op jit(solution)/shard_map/ppermute | solution.py:48
  102.7 4.0 %collective-permute-start.28 = (f32[64,128]{1,0:T(8,128)S(1)}, f32[64,128]{1,0:T(8,128)S(1)}, u32[]{:S(2)}, u32[]{:S(2)}) collective-permute-start(f32[64,128]{1,0:T(8,128)S(1)} %constant_dynamic-update-slice_fusion.8.refs_4_), channel_id=1, source_target_pairs={{0,2},{2,0},{1,3},{3,1},{4,6},{6,4},{5,7},{7,5},{8,10},{10,8},{9,1... | collective-permute-start | bytes 98312 | tf_op jit(solution)/shard_map/ppermute | solution.py:48
  104.6 2.1 %collective-permute-start.27 = (f32[64,128]{1,0:T(8,128)S(1)}, f32[64,128]{1,0:T(8,128)S(1)}, u32[]{:S(2)}, u32[]{:S(2)}) collective-permute-start(f32[64,128]{1,0:T(8,128)S(1)} %constant_dynamic-update-slice_fusion.8.refs_4_), channel_id=1, source_target_pairs={{0,1},{1,0},{2,3},{3,2},{4,5},{5,4},{6,7},{7,6},{8,9},{9,8},{10,11... | collective-permute-start | bytes 98312 | tf_op jit(solution)/shard_map/ppermute | solution.py:48
  106.7 1.2 %collective-permute-start.29 = (f32[64,128]{1,0:T(8,128)S(1)}, f32[64,128]{1,0:T(8,128)S(1)}, u32[]{:S(2)}, u32[]{:S(2)}) collective-permute-start(f32[64,128]{1,0:T(8,128)S(1)} %collective-permute-done.28.refs_6_), channel_id=1, source_target_pairs={{0,1},{1,0},{2,3},{3,2},{4,5},{5,4},{6,7},{7,6},{8,9},{9,8},{10,11... | collective-permute-start | bytes 98312 | tf_op jit(solution)/shard_map/ppermute | solution.py:48

commit v3 on v2

--- a/solution.py
+++ b/solution.py
@@ -192,7 +192,7 @@
 
 def taper_of(squared):
     squared = jnp.maximum(squared, 1e-20)
-    remain = jnp.maximum(4.0 - squared * lax.rsqrt(squared), 0.0)
+    remain = jnp.maximum(4.0 - jnp.exp(0.5 * jnp.log(squared)), 0.0)
     twice = remain * remain
     return twice * twice * (5.0 - remain)
 

time: 110 us -> 109 us (level)
  the two profiles are of different devices: /device:TPU:0 before, /device:TPU:5 now
where the time goes in v3:
time: 109 us; the launch traced here: 111 us
  Pallas kernels  51.9 us (48%)
  starting transfers between devices  43 us (39%)
  waiting for transfers between devices  12.4 us (11%)
  other arithmetic  1.48 us (1%)
  between operations  1.43 us (1%)
    pallas_call x6, Pallas kernels, call(): pl.pallas_call(kernel, in_specs=in_specs, out_shape=shapes, out_specs=out...  51.9 us
    ppermute x30, starting transfers between devices, swap(): lax.ppermute(x, axis, [(i, i ^ code) for i in range(lax.axis_size(axis))])  43 us
    ppermute x30, waiting for transfers between devices, swap(): lax.ppermute(x, axis, [(i, i ^ code) for i in range(lax.axis_size(axis))])  12.4 us
  transfers between devices with their start and end apart: 30, of which 14 were waited for; matrix products, arithmetic and copies ran while one was open for 2% of the time, Pallas kernels for 4%

profile of v3, /device:TPU:5, one launch (start us, length us, event | category | flops | bytes accessed | tf_op | source)
XLA Modules:
  0.0 111.1 jit_solution(14982376792099200715)
XLA Ops:
  1.3 0.7 broadcast_select_fusion
  2.0 3.3 %collective-permute-start.2 = (s32[4,128]{1,0:T(4,128)S(1)}, s32[4,128]{1,0:T(4,128)S(1)}, u32[]{:S(2)}, u32[]{:S(2)}) collective-permute-start(s32[4,128]{1,0:T(4,128)S(1)} %reshape.28), channel_id=1, source_target_pairs={{0,12},{4,8},{8,4},{12,0},{1,13},{5,9},{9,5},{13,1},{2,14},{6,10},... | collective-permute-start | bytes 6152 | tf_op jit(solution)/shard_map/ppermute | solution.py:48
  5.3 0.3 collective-permute-start
  5.7 1.0 copy.9
  6.6 0.8 fusion
  7.4 3.3 %collective-permute-start.8 = (f32[256,128]{1,0:T(8,128)S(1)}, f32[256,128]{1,0:T(8,128)S(1)}, u32[]{:S(2)}, u32[]{:S(2)}) collective-permute-start(f32[256,128]{1,0:T(8,128)S(1)} %bitcast.22), channel_id=1, source_target_pairs={{0,12},{4,8},{8,4},{12,0},{1,13},{5,9},{9,5},{13,1},{2,14},{6,10},... | collective-permute-start | bytes 393224 | tf_op jit(solution)/shard_map/ppermute | solution.py:48
  10.7 0.4 collective-permute-start.6
  11.1 1.3 %collective-permute-start.4 = (s32[16,128]{1,0:T(8,128)S(1)}, s32[16,128]{1,0:T(8,128)S(1)}, u32[]{:S(2)}, u32[]{:S(2)}) collective-permute-start(s32[16,128]{1,0:T(8,128)S(1)} %pad_add_fusion.refs_0_), channel_id=1, source_target_pairs={{0,2},{2,0},{1,3},{3,1},{4,6},{6,4},{5,7},{7,5},{8,10},{10,8},{9,1... | collective-permute-start | bytes 24584 | tf_op jit(solution)/shard_map/ppermute | solution.py:48
  12.3 2.5 %collective-permute-start.3 = (s32[16,128]{1,0:T(8,128)S(1)}, s32[16,128]{1,0:T(8,128)S(1)}, u32[]{:S(2)}, u32[]{:S(2)}) collective-permute-start(s32[16,128]{1,0:T(8,128)S(1)} %pad_add_fusion.refs_0_), channel_id=1, source_target_pairs={{0,1},{1,0},{2,3},{3,2},{4,5},{5,4},{6,7},{7,6},{8,9},{9,8},{10,11... | collective-permute-start | bytes 24584 | tf_op jit(solution)/shard_map/ppermute | solution.py:48
  14.8 2.2 %collective-permute-start.5 = (s32[16,128]{1,0:T(8,128)S(1)}, s32[16,128]{1,0:T(8,128)S(1)}, u32[]{:S(2)}, u32[]{:S(2)}) collective-permute-start(s32[16,128]{1,0:T(8,128)S(1)} %collective-permute-done.4.refs_2_), channel_id=1, source_target_pairs={{0,1},{1,0},{2,3},{3,2},{4,5},{5,4},{6,7},{7,6},{8,9},{9,8},{10,11... | collective-permute-start | bytes 24584 | tf_op jit(solution)/shard_map/ppermute | solution.py:48
  17.0 0.4 shard_map.69.refs_2_
  17.4 0.5 collective-permute-done.5.refs_3_
  17.8 3.8 %shard_map.68 = (s32[16,128]{1,0:T(8,128)S(1)}, s32[1]{0:T(128)}) custom-call(s32[16,128]{1,0:T(8,128)S(1)} %pad_add_fusion.refs_0_, s32[16,128]{1,0:T(8,128)S(1)} %collective-permute-done.3.refs_1_, s32[16,128]{1,0:T(8,128)S(1)} %collective-permute-done.4.refs_2_, s32[16,128]{1,0:T(8,128)S(1)} %collective-permute-done.5.refs_3_), custom_call_target="tpu_custom_call" | custom-call | flops 10000000 | bytes 1048576 | tf_op jit(solution)/shard_map/pallas_call | solution.py:404
  21.7 0.9 collective-permute-start.9
  22.7 0.0 collective-permute-start.10
  22.7 0.5 collective-permute-start.11
  23.2 0.5 collective-permute-done.9.refs_7_
  23.6 0.4 collective-permute-done.10.refs_9_
  24.0 0.2 collective-permute-done.11.refs_11_
  24.2 32.4 %shard_map.70 = (f32[14336,128]{1,0:T(8,128)S(1)}, f32[14336,128]{1,0:T(8,128)S(1)}, f32[14336,128]{1,0:T(8,128)S(1)}, f32[14336,128]{1,0:T(8,128)S(1)}, bf16[24...) custom-call(s32[2048]{0:T(1024)S(1)} %bitcast.16, ...), custom_call_target="tpu_custom_call" | custom-call | flops 100000000 | bytes 1048576 | tf_op jit(solution)/shard_map/pallas_call | solution.py:404
  56.6 3.1 %collective-permute-start.14 = (f32[32,128]{1,0:T(8,128)S(1)}, f32[32,128]{1,0:T(8,128)S(1)}, u32[]{:S(2)}, u32[]{:S(2)}) collective-permute-start(f32[32,128]{1,0:T(8,128)S(1)} %get-tuple-element.42), channel_id=1, source_target_pairs={{0,12},{4,8},{8,4},{12,0},{1,13},{5,9},{9,5},{13,1},{2,14},{6,10},... | collective-permute-start | bytes 49160 | tf_op jit(solution)/shard_map/ppermute | solution.py:48
  59.7 0.5 collective-permute-start.12
  60.2 2.4 %collective-permute-done.12 = f32[32,128]{1,0:T(8,128)S(1)} collective-permute-done((f32[32,128]{1,0:T(8,128)S(1)}, f32[32,128]{1,0:T(8,128)S(1)}, u32[]{:S(2)}, u32[]{:S(2)}) %collective-permute-start.12) | collective-permute-done | bytes 16416 | tf_op jit(solution)/shard_map/ppermute | solution.py:48
  62.6 0.9 collective-permute-done.13
  63.5 3.2 %collective-permute-start.16 = (f32[128,128]{1,0:T(8,128)S(1)}, f32[128,128]{1,0:T(8,128)S(1)}, u32[]{:S(2)}, u32[]{:S(2)}) collective-permute-start(f32[128,128]{1,0:T(8,128)S(1)} %constant_dynamic-update-slice_fusion.refs_9_), channel_id=1, source_target_pairs={{0,2},{2,0},{1,3},{3,1},{4,6},{6,4},{5,7},{7,5},{8,10},{10,8},{9,1... | collective-permute-start | bytes 196616 | tf_op jit(solution)/shard_map/ppermute | solution.py:48
  66.7 0.7 collective-permute-start.15
  67.4 0.9 collective-permute-done.16.refs_11_
  68.3 2.8 %collective-permute-start.17 = (f32[128,128]{1,0:T(8,128)S(1)}, f32[128,128]{1,0:T(8,128)S(1)}, u32[]{:S(2)}, u32[]{:S(2)}) collective-permute-start(f32[128,128]{1,0:T(8,128)S(1)} %collective-permute-done.16.refs_11_), channel_id=1, source_target_pairs={{0,1},{1,0},{2,3},{3,2},{4,5},{5,4},{6,7},{7,6},{8,9},{9,8},{10,11... | collective-permute-start | bytes 196616 | tf_op jit(solution)/shard_map/ppermute | solution.py:48
  71.1 0.9 collective-permute-done.17.refs_12_
  72.0 7.2 %shard_map.71 = (f32[32,128]{1,0:T(8,128)S(1)}, f32[8,128]{1,0:T(8,128)S(1)}, f32[128,128]{1,0:T(8,128)S(1)}, f32[512,128]{1,0:T(8,128)S(1)}, f32[512,128]{1,0:T(8,128)S(1)}) custom-call(s32[2048]{0:T(1024)S(1)} %bitcast.17, s32[1]{0:T(128)} %get-tuple-element.33.refs_1_, bf16[4224,128]{1,0:T(8,128)(2,1)S(1)} %shard_map.69.refs_2_, ...), custom_call_target="tpu_custom_call" | custom-call | flops 100000000 | bytes 1048576 | tf_op jit(solution)/shard_map/pallas_call | solution.py:404
  79.2 1.3 %collective-permute-start.20 = (f32[32,128]{1,0:T(8,128)S(1)}, f32[32,128]{1,0:T(8,128)S(1)}, u32[]{:S(2)}, u32[]{:S(2)}) collective-permute-start(f32[32,128]{1,0:T(8,128)S(1)} %get-tuple-element.51), channel_id=1, source_target_pairs={{0,12},{4,8},{8,4},{12,0},{1,13},{5,9},{9,5},{13,1},{2,14},{6,10},... | collective-permute-start | bytes 49160 | tf_op jit(solution)/shard_map/ppermute | solution.py:48
  80.5 2.3 %collective-permute-start.18 = (f32[32,128]{1,0:T(8,128)S(1)}, f32[32,128]{1,0:T(8,128)S(1)}, u32[]{:S(2)}, u32[]{:S(2)}) collective-permute-start(f32[32,128]{1,0:T(8,128)S(1)} %get-tuple-element.51), channel_id=1, source_target_pairs={{0,4},{4,0},{8,12},{12,8},{1,5},{5,1},{9,13},{13,9},{2,6},{6,2},{1... | collective-permute-start | bytes 49160 | tf_op jit(solution)/shard_map/ppermute | solution.py:48
  82.8 1.5 %collective-permute-done.18 = f32[32,128]{1,0:T(8,128)S(1)} collective-permute-done((f32[32,128]{1,0:T(8,128)S(1)}, f32[32,128]{1,0:T(8,128)S(1)}, u32[]{:S(2)}, u32[]{:S(2)}) %collective-permute-start.18) | collective-permute-done | bytes 16416 | tf_op jit(solution)/shard_map/ppermute | solution.py:48
  84.3 0.4 collective-permute-start.22
  84.7 1.9 %collective-permute-start.21 = (f32[128,128]{1,0:T(8,128)S(1)}, f32[128,128]{1,0:T(8,128)S(1)}, u32[]{:S(2)}, u32[]{:S(2)}) collective-permute-start(f32[128,128]{1,0:T(8,128)S(1)} %constant_dynamic-update-slice_fusion.4.refs_9_), channel_id=1, source_target_pairs={{0,1},{1,0},{2,3},{3,2},{4,5},{5,4},{6,7},{7,6},{8,9},{9,8},{10,11... | collective-permute-start | bytes 196616 | tf_op jit(solution)/shard_map/ppermute | solution.py:48
  86.6 0.9 collective-permute-done.22.refs_11_
  87.5 2.9 %collective-permute-start.23 = (f32[128,128]{1,0:T(8,128)S(1)}, f32[128,128]{1,0:T(8,128)S(1)}, u32[]{:S(2)}, u32[]{:S(2)}) collective-permute-start(f32[128,128]{1,0:T(8,128)S(1)} %collective-permute-done.22.refs_11_), channel_id=1, source_target_pairs={{0,1},{1,0},{2,3},{3,2},{4,5},{5,4},{6,7},{7,6},{8,9},{9,8},{10,11... | collective-permute-start | bytes 196616 | tf_op jit(solution)/shard_map/ppermute | solution.py:48
  90.4 0.9 collective-permute-done.23.refs_12_
  91.3 7.3 %shard_map.72 = (f32[32,128]{1,0:T(8,128)S(1)}, f32[8,128]{1,0:T(8,128)S(1)}, f32[128,128]{1,0:T(8,128)S(1)}, f32[128,128]{1,0:T(8,128)S(1)}, f32[128,128]{1,0:T(8,128)S(1)}, /*index=5*/f32[8,128]{1,0:T(8,128)S(1)}) custom-call(s32[2048]{0:T(1024)S(1)} %bitcast.18, s32[1]{0:T(128)} %get-tuple-element.33.refs_1_, bf16[4224,128]{1,0:T(8,128)(2,1)S(1)} %shard_map.69.refs_2_, ...), custom_call_target="tpu_custom_call" | custom-call | flops 100000000 | bytes 1048576 | tf_op jit(solution)/shard_map/pallas_call | solution.py:404
  98.7 1.5 %collective-permute-start.26 = (f32[8,128]{1,0:T(8,128)S(1)}, f32[8,128]{1,0:T(8,128)S(1)}, u32[]{:S(2)}, u32[]{:S(2)}) collective-permute-start(f32[8,128]{1,0:T(8,128)S(1)} %get-tuple-element.57), channel_id=1, source_target_pairs={{0,12},{4,8},{8,4},{12,0},{1,13},{5,9},{9,5},{13,1},{2,14},{6,10},... | collective-permute-start | bytes 12296 | tf_op jit(solution)/shard_map/ppermute | solution.py:48
  100.1 2.2 %collective-permute-start.24 = (f32[8,128]{1,0:T(8,128)S(1)}, f32[8,128]{1,0:T(8,128)S(1)}, u32[]{:S(2)}, u32[]{:S(2)}) collective-permute-start(f32[8,128]{1,0:T(8,128)S(1)} %get-tuple-element.57), channel_id=1, source_target_pairs={{0,4},{4,0},{8,12},{12,8},{1,5},{5,1},{9,13},{13,9},{2,6},{6,2},{1... | collective-permute-start | bytes 12296 | tf_op jit(solution)/shard_map/ppermute | solution.py:48
  102.3 1.2 %collective-permute-done.24 = f32[8,128]{1,0:T(8,128)S(1)} collective-permute-done((f32[8,128]{1,0:T(8,128)S(1)}, f32[8,128]{1,0:T(8,128)S(1)}, u32[]{:S(2)}, u32[]{:S(2)}) %collective-permute-start.24) | collective-permute-done | bytes 4128 | tf_op jit(solution)/shard_map/ppermute | solution.py:48
  103.5 0.5 collective-permute-start.28
  104.0 1.9 %collective-permute-start.27 = (f32[64,128]{1,0:T(8,128)S(1)}, f32[64,128]{1,0:T(8,128)S(1)}, u32[]{:S(2)}, u32[]{:S(2)}) collective-permute-start(f32[64,128]{1,0:T(8,128)S(1)} %constant_dynamic-update-slice_fusion.8.refs_4_), channel_id=1, source_target_pairs={{0,1},{1,0},{2,3},{3,2},{4,5},{5,4},{6,7},{7,6},{8,9},{9,8},{10,11... | collective-permute-start | bytes 98312 | tf_op jit(solution)/shard_map/ppermute | solution.py:48
  105.9 0.4 collective-permute-done.28.refs_6_
  106.4 3.2 %collective-permute-start.29 = (f32[64,128]{1,0:T(8,128)S(1)}, f32[64,128]{1,0:T(8,128)S(1)}, u32[]{:S(2)}, u32[]{:S(2)}) collective-permute-start(f32[64,128]{1,0:T(8,128)S(1)} %collective-permute-done.28.refs_6_), channel_id=1, source_target_pairs={{0,1},{1,0},{2,3},{3,2},{4,5},{5,4},{6,7},{7,6},{8,9},{9,8},{10,11... | collective-permute-start | bytes 98312 | tf_op jit(solution)/shard_map/ppermute | solution.py:48
  109.5 0.9 collective-permute-done.29.refs_7_
  110.4 0.7 shard_map.73
  (37 shorter events, 0.1 us)
Async XLA Ops:
  2.0 8.7 %collective-permute-start.2 = (s32[4,128]{1,0:T(4,128)S(1)}, s32[4,128]{1,0:T(4,128)S(1)}, u32[]{:S(2)}, u32[]{:S(2)}) collective-permute-start(s32[4,128]{1,0:T(4,128)S(1)} %reshape.28), channel_id=1, source_target_pairs={{0,12},{4,8},{8,4},{12,0},{1,13},{5,9},{9,5},{13,1},{2,14},{6,10},... | collective-permute-start | bytes 6152 | tf_op jit(solution)/shard_map/ppermute | solution.py:48
  5.3 5.7 %collective-permute-start.1 = (s32[4,128]{1,0:T(4,128)S(1)}, s32[4,128]{1,0:T(4,128)S(1)}, u32[]{:S(2)}, u32[]{:S(2)}) collective-permute-start(s32[4,128]{1,0:T(4,128)S(1)} %reshape.28), channel_id=1, source_target_pairs={{0,8},{4,12},{8,0},{12,4},{1,9},{5,13},{9,1},{13,5},{2,10},{6,14},... | collective-permute-start | bytes 6152 | tf_op jit(solution)/shard_map/ppermute | solution.py:48
  5.3 5.7 %collective-permute-start = (s32[4,128]{1,0:T(4,128)S(1)}, s32[4,128]{1,0:T(4,128)S(1)}, u32[]{:S(2)}, u32[]{:S(2)}) collective-permute-start(s32[4,128]{1,0:T(4,128)S(1)} %reshape.28), channel_id=1, source_target_pairs={{0,4},{4,0},{8,12},{12,8},{1,5},{5,1},{9,13},{13,9},{2,6},{6,2},{1... | collective-permute-start | bytes 6152 | tf_op jit(solution)/shard_map/ppermute | solution.py:48
  7.4 14.3 %collective-permute-start.8 = (f32[256,128]{1,0:T(8,128)S(1)}, f32[256,128]{1,0:T(8,128)S(1)}, u32[]{:S(2)}, u32[]{:S(2)}) collective-permute-start(f32[256,128]{1,0:T(8,128)S(1)} %bitcast.22), channel_id=1, source_target_pairs={{0,12},{4,8},{8,4},{12,0},{1,13},{5,9},{9,5},{13,1},{2,14},{6,10},... | collective-permute-start | bytes 393224 | tf_op jit(solution)/shard_map/ppermute | solution.py:48
  10.7 11.0 %collective-permute-start.7 = (f32[256,128]{1,0:T(8,128)S(1)}, f32[256,128]{1,0:T(8,128)S(1)}, u32[]{:S(2)}, u32[]{:S(2)}) collective-permute-start(f32[256,128]{1,0:T(8,128)S(1)} %bitcast.23), channel_id=1, source_target_pairs={{0,8},{4,12},{8,0},{12,4},{1,9},{5,13},{9,1},{13,5},{2,10},{6,14},... | collective-permute-start | bytes 393224 | tf_op jit(solution)/shard_map/ppermute | solution.py:48
  10.7 11.0 %collective-permute-start.6 = (f32[256,128]{1,0:T(8,128)S(1)}, f32[256,128]{1,0:T(8,128)S(1)}, u32[]{:S(2)}, u32[]{:S(2)}) collective-permute-start(f32[256,128]{1,0:T(8,128)S(1)} %bitcast.24), channel_id=1, source_target_pairs={{0,4},{4,0},{8,12},{12,8},{1,5},{5,1},{9,13},{13,9},{2,6},{6,2},{1... | collective-permute-start | bytes 393224 | tf_op jit(solution)/shard_map/ppermute | solution.py:48
  11.1 3.8 %collective-permute-start.4 = (s32[16,128]{1,0:T(8,128)S(1)}, s32[16,128]{1,0:T(8,128)S(1)}, u32[]{:S(2)}, u32[]{:S(2)}) collective-permute-start(s32[16,128]{1,0:T(8,128)S(1)} %pad_add_fusion.refs_0_), channel_id=1, source_target_pairs={{0,2},{2,0},{1,3},{3,1},{4,6},{6,4},{5,7},{7,5},{8,10},{10,8},{9,1... | collective-permute-start | bytes 24584 | tf_op jit(solution)/shard_map/ppermute | solution.py:48
  12.3 5.0 %collective-permute-start.3 = (s32[16,128]{1,0:T(8,128)S(1)}, s32[16,128]{1,0:T(8,128)S(1)}, u32[]{:S(2)}, u32[]{:S(2)}) collective-permute-start(s32[16,128]{1,0:T(8,128)S(1)} %pad_add_fusion.refs_0_), channel_id=1, source_target_pairs={{0,1},{1,0},{2,3},{3,2},{4,5},{5,4},{6,7},{7,6},{8,9},{9,8},{10,11... | collective-permute-start | bytes 24584 | tf_op jit(solution)/shard_map/ppermute | solution.py:48
  14.8 3.0 %collective-permute-start.5 = (s32[16,128]{1,0:T(8,128)S(1)}, s32[16,128]{1,0:T(8,128)S(1)}, u32[]{:S(2)}, u32[]{:S(2)}) collective-permute-start(s32[16,128]{1,0:T(8,128)S(1)} %collective-permute-done.4.refs_2_), channel_id=1, source_target_pairs={{0,1},{1,0},{2,3},{3,2},{4,5},{5,4},{6,7},{7,6},{8,9},{9,8},{10,11... | collective-permute-start | bytes 24584 | tf_op jit(solution)/shard_map/ppermute | solution.py:48
  21.7 1.9 %collective-permute-start.9 = (f32[256,128]{1,0:T(8,128)S(1)}, f32[256,128]{1,0:T(8,128)S(1)}, u32[]{:S(2)}, u32[]{:S(2)}) collective-permute-start(f32[256,128]{1,0:T(8,128)S(1)} %collective-permute-done.6.refs_6_), channel_id=1, source_target_pairs={{0,1},{1,0},{2,3},{3,2},{4,5},{5,4},{6,7},{7,6},{8,9},{9,8},{10,11... | collective-permute-start | bytes 393224 | tf_op jit(solution)/shard_map/ppermute | solution.py:48
  22.7 1.3 %collective-permute-start.10 = (f32[256,128]{1,0:T(8,128)S(1)}, f32[256,128]{1,0:T(8,128)S(1)}, u32[]{:S(2)}, u32[]{:S(2)}) collective-permute-start(f32[256,128]{1,0:T(8,128)S(1)} %collective-permute-done.7.refs_8_), channel_id=1, source_target_pairs={{0,1},{1,0},{2,3},{3,2},{4,5},{5,4},{6,7},{7,6},{8,9},{9,8},{10,11... | collective-permute-start | bytes 393224 | tf_op jit(solution)/shard_map/ppermute | solution.py:48
  22.7 1.5 %collective-permute-start.11 = (f32[256,128]{1,0:T(8,128)S(1)}, f32[256,128]{1,0:T(8,128)S(1)}, u32[]{:S(2)}, u32[]{:S(2)}) collective-permute-start(f32[256,128]{1,0:T(8,128)S(1)} %collective-permute-done.8.refs_10_), channel_id=1, source_target_pairs={{0,1},{1,0},{2,3},{3,2},{4,5},{5,4},{6,7},{7,6},{8,9},{9,8},{10,11... | collective-permute-start | bytes 393224 | tf_op jit(solution)/shard_map/ppermute | solution.py:48
  56.6 6.9 %collective-permute-start.14 = (f32[32,128]{1,0:T(8,128)S(1)}, f32[32,128]{1,0:T(8,128)S(1)}, u32[]{:S(2)}, u32[]{:S(2)}) collective-permute-start(f32[32,128]{1,0:T(8,128)S(1)} %get-tuple-element.42), channel_id=1, source_target_pairs={{0,12},{4,8},{8,4},{12,0},{1,13},{5,9},{9,5},{13,1},{2,14},{6,10},... | collective-permute-start | bytes 49160 | tf_op jit(solution)/shard_map/ppermute | solution.py:48
  59.7 3.7 %collective-permute-start.13 = (f32[32,128]{1,0:T(8,128)S(1)}, f32[32,128]{1,0:T(8,128)S(1)}, u32[]{:S(2)}, u32[]{:S(2)}) collective-permute-start(f32[32,128]{1,0:T(8,128)S(1)} %get-tuple-element.42), channel_id=1, source_target_pairs={{0,8},{4,12},{8,0},{12,4},{1,9},{5,13},{9,1},{13,5},{2,10},{6,14},... | collective-permute-start | bytes 49160 | tf_op jit(solution)/shard_map/ppermute | solution.py:48
  59.7 2.9 %collective-permute-start.12 = (f32[32,128]{1,0:T(8,128)S(1)}, f32[32,128]{1,0:T(8,128)S(1)}, u32[]{:S(2)}, u32[]{:S(2)}) collective-permute-start(f32[32,128]{1,0:T(8,128)S(1)} %get-tuple-element.42), channel_id=1, source_target_pairs={{0,4},{4,0},{8,12},{12,8},{1,5},{5,1},{9,13},{13,9},{2,6},{6,2},{1... | collective-permute-start | bytes 49160 | tf_op jit(solution)/shard_map/ppermute | solution.py:48
  63.5 4.8 %collective-permute-start.16 = (f32[128,128]{1,0:T(8,128)S(1)}, f32[128,128]{1,0:T(8,128)S(1)}, u32[]{:S(2)}, u32[]{:S(2)}) collective-permute-start(f32[128,128]{1,0:T(8,128)S(1)} %constant_dynamic-update-slice_fusion.refs_9_), channel_id=1, source_target_pairs={{0,2},{2,0},{1,3},{3,1},{4,6},{6,4},{5,7},{7,5},{8,10},{10,8},{9,1... | collective-permute-start | bytes 196616 | tf_op jit(solution)/shard_map/ppermute | solution.py:48
  66.7 4.4 %collective-permute-start.15 = (f32[128,128]{1,0:T(8,128)S(1)}, f32[128,128]{1,0:T(8,128)S(1)}, u32[]{:S(2)}, u32[]{:S(2)}) collective-permute-start(f32[128,128]{1,0:T(8,128)S(1)} %constant_dynamic-update-slice_fusion.refs_9_), channel_id=1, source_target_pairs={{0,1},{1,0},{2,3},{3,2},{4,5},{5,4},{6,7},{7,6},{8,9},{9,8},{10,11... | collective-permute-start | bytes 196616 | tf_op jit(solution)/shard_map/ppermute | solution.py:48
  68.3 3.7 %collective-permute-start.17 = (f32[128,128]{1,0:T(8,128)S(1)}, f32[128,128]{1,0:T(8,128)S(1)}, u32[]{:S(2)}, u32[]{:S(2)}) collective-permute-start(f32[128,128]{1,0:T(8,128)S(1)} %collective-permute-done.16.refs_11_), channel_id=1, source_target_pairs={{0,1},{1,0},{2,3},{3,2},{4,5},{5,4},{6,7},{7,6},{8,9},{9,8},{10,11... | collective-permute-start | bytes 196616 | tf_op jit(solution)/shard_map/ppermute | solution.py:48
  79.2 5.1 %collective-permute-start.20 = (f32[32,128]{1,0:T(8,128)S(1)}, f32[32,128]{1,0:T(8,128)S(1)}, u32[]{:S(2)}, u32[]{:S(2)}) collective-permute-start(f32[32,128]{1,0:T(8,128)S(1)} %get-tuple-element.51), channel_id=1, source_target_pairs={{0,12},{4,8},{8,4},{12,0},{1,13},{5,9},{9,5},{13,1},{2,14},{6,10},... | collective-permute-start | bytes 49160 | tf_op jit(solution)/shard_map/ppermute | solution.py:48
  80.5 3.8 %collective-permute-start.19 = (f32[32,128]{1,0:T(8,128)S(1)}, f32[32,128]{1,0:T(8,128)S(1)}, u32[]{:S(2)}, u32[]{:S(2)}) collective-permute-start(f32[32,128]{1,0:T(8,128)S(1)} %get-tuple-element.51), channel_id=1, source_target_pairs={{0,8},{4,12},{8,0},{12,4},{1,9},{5,13},{9,1},{13,5},{2,10},{6,14},... | collective-permute-start | bytes 49160 | tf_op jit(solution)/shard_map/ppermute | solution.py:48
  80.5 3.8 %collective-permute-start.18 = (f32[32,128]{1,0:T(8,128)S(1)}, f32[32,128]{1,0:T(8,128)S(1)}, u32[]{:S(2)}, u32[]{:S(2)}) collective-permute-start(f32[32,128]{1,0:T(8,128)S(1)} %get-tuple-element.51), channel_id=1, source_target_pairs={{0,4},{4,0},{8,12},{12,8},{1,5},{5,1},{9,13},{13,9},{2,6},{6,2},{1... | collective-permute-start | bytes 49160 | tf_op jit(solution)/shard_map/ppermute | solution.py:48
  84.3 3.2 %collective-permute-start.22 = (f32[128,128]{1,0:T(8,128)S(1)}, f32[128,128]{1,0:T(8,128)S(1)}, u32[]{:S(2)}, u32[]{:S(2)}) collective-permute-start(f32[128,128]{1,0:T(8,128)S(1)} %constant_dynamic-update-slice_fusion.4.refs_9_), channel_id=1, source_target_pairs={{0,2},{2,0},{1,3},{3,1},{4,6},{6,4},{5,7},{7,5},{8,10},{10,8},{9,1... | collective-permute-start | bytes 196616 | tf_op jit(solution)/shard_map/ppermute | solution.py:48
  84.7 5.7 %collective-permute-start.21 = (f32[128,128]{1,0:T(8,128)S(1)}, f32[128,128]{1,0:T(8,128)S(1)}, u32[]{:S(2)}, u32[]{:S(2)}) collective-permute-start(f32[128,128]{1,0:T(8,128)S(1)} %constant_dynamic-update-slice_fusion.4.refs_9_), channel_id=1, source_target_pairs={{0,1},{1,0},{2,3},{3,2},{4,5},{5,4},{6,7},{7,6},{8,9},{9,8},{10,11... | collective-permute-start | bytes 196616 | tf_op jit(solution)/shard_map/ppermute | solution.py:48
  87.5 3.8 %collective-permute-start.23 = (f32[128,128]{1,0:T(8,128)S(1)}, f32[128,128]{1,0:T(8,128)S(1)}, u32[]{:S(2)}, u32[]{:S(2)}) collective-permute-start(f32[128,128]{1,0:T(8,128)S(1)} %collective-permute-done.22.refs_11_), channel_id=1, source_target_pairs={{0,1},{1,0},{2,3},{3,2},{4,5},{5,4},{6,7},{7,6},{8,9},{9,8},{10,11... | collective-permute-start | bytes 196616 | tf_op jit(solution)/shard_map/ppermute | solution.py:48
  98.7 4.8 %collective-permute-start.26 = (f32[8,128]{1,0:T(8,128)S(1)}, f32[8,128]{1,0:T(8,128)S(1)}, u32[]{:S(2)}, u32[]{:S(2)}) collective-permute-start(f32[8,128]{1,0:T(8,128)S(1)} %get-tuple-element.57), channel_id=1, source_target_pairs={{0,12},{4,8},{8,4},{12,0},{1,13},{5,9},{9,5},{13,1},{2,14},{6,10},... | collective-permute-start | bytes 12296 | tf_op jit(solution)/shard_map/ppermute | solution.py:48
  100.1 3.4 %collective-permute-start.25 = (f32[8,128]{1,0:T(8,128)S(1)}, f32[8,128]{1,0:T(8,128)S(1)}, u32[]{:S(2)}, u32[]{:S(2)}) collective-permute-start(f32[8,128]{1,0:T(8,128)S(1)} %get-tuple-element.57), channel_id=1, source_target_pairs={{0,8},{4,12},{8,0},{12,4},{1,9},{5,13},{9,1},{13,5},{2,10},{6,14},... | collective-permute-start | bytes 12296 | tf_op jit(solution)/shard_map/ppermute | solution.py:48
  100.1 3.4 %collective-permute-start.24 = (f32[8,128]{1,0:T(8,128)S(1)}, f32[8,128]{1,0:T(8,128)S(1)}, u32[]{:S(2)}, u32[]{:S(2)}) collective-permute-start(f32[8,128]{1,0:T(8,128)S(1)} %get-tuple-element.57), channel_id=1, source_target_pairs={{0,4},{4,0},{8,12},{12,8},{1,5},{5,1},{9,13},{13,9},{2,6},{6,2},{1... | collective-permute-start | bytes 12296 | tf_op jit(solution)/shard_map/ppermute | solution.py:48
  103.5 2.8 %collective-permute-start.28 = (f32[64,128]{1,0:T(8,128)S(1)}, f32[64,128]{1,0:T(8,128)S(1)}, u32[]{:S(2)}, u32[]{:S(2)}) collective-permute-start(f32[64,128]{1,0:T(8,128)S(1)} %constant_dynamic-update-slice_fusion.8.refs_4_), channel_id=1, source_target_pairs={{0,2},{2,0},{1,3},{3,1},{4,6},{6,4},{5,7},{7,5},{8,10},{10,8},{9,1... | collective-permute-start | bytes 98312 | tf_op jit(solution)/shard_map/ppermute | solution.py:48
  104.0 5.5 %collective-permute-start.27 = (f32[64,128]{1,0:T(8,128)S(1)}, f32[64,128]{1,0:T(8,128)S(1)}, u32[]{:S(2)}, u32[]{:S(2)}) collective-permute-start(f32[64,128]{1,0:T(8,128)S(1)} %constant_dynamic-update-slice_fusion.8.refs_4_), channel_id=1, source_target_pairs={{0,1},{1,0},{2,3},{3,2},{4,5},{5,4},{6,7},{7,6},{8,9},{9,8},{10,11... | collective-permute-start | bytes 98312 | tf_op jit(solution)/shard_map/ppermute | solution.py:48
  106.4 4.0 %collective-permute-start.29 = (f32[64,128]{1,0:T(8,128)S(1)}, f32[64,128]{1,0:T(8,128)S(1)}, u32[]{:S(2)}, u32[]{:S(2)}) collective-permute-start(f32[64,128]{1,0:T(8,128)S(1)} %collective-permute-done.28.refs_6_), channel_id=1, source_target_pairs={{0,1},{1,0},{2,3},{3,2},{4,5},{5,4},{6,7},{7,6},{8,9},{9,8},{10,11... | collective-permute-start | bytes 98312 | tf_op jit(solution)/shard_map/ppermute | solution.py:48
